TPU v7x, 32 devices: a whole 2x2x4 slice. The times are simulated.
32 devices in a mesh: pipe: 4 (over y, x), expert: 8 (over z, core).
Axes of the slice: x: 2, y: 2, z: 4, core: 2. Of those that a mesh axis runs over, the one named last changes fastest.
Arguments:
- fwd_acts: bfloat16 [4, 1024, 3584], P('pipe', 'expert'), may hold values from -6 to 6
- bwd_saved: bfloat16 [4, 1024, 3584], P('pipe', 'expert'), may hold values from -6 to 6
- bwd_grads: bfloat16 [4, 1024, 3584], P('pipe', 'expert'), may hold values from -6 to 6
- norm_gain: float32 [4, 3584], P('pipe'), may hold values from 0.1 to 1.9
- router: bfloat16 [4, 3584, 4], P('pipe'), may hold values from -0.09375 to 0.09375
- w_up: bfloat16 [4, 3584, 4096], P('pipe', None, 'expert'), may hold values from -0.09375 to 0.09375
- w_down: bfloat16 [4, 4096, 3584], P('pipe', 'expert'), may hold values from -0.1875 to 0.1875
- fwd_experts: int32 [4, 1024, 2], P('pipe', 'expert'), may hold values from 0 to 3, all different within a row; in each aligned block of 128 rows (0 to 127, 128 to 255, ..., all dimensions but the last counted through in order) at most 72 rows name the same one
- bwd_experts: int32 [4, 1024, 2], P('pipe', 'expert'), may hold values from 0 to 3, all different within a row; in each aligned block of 128 rows (0 to 127, 128 to 255, ..., all dimensions but the last counted through in order) at most 72 rows name the same one
Outputs:
- fwd_next: bfloat16 [4, 1024, 3584], P('pipe', 'expert')
- bwd_next: bfloat16 [4, 1024, 3584], P('pipe', 'expert')
Inputs may be any that keep to these rules, and one draw needn't show every extreme that they name: `fwd_experts`: each row names 2 different experts. Within the 128 rows of one device no expert is named by more than 72 rows, and in every draw some expert is named by exactly 72 rows of some device. `bwd_experts`: each row names 2 different experts. Within the 128 rows of one device no expert is named by more than 72 rows, and in every draw some expert is named by exactly 72 rows of some device.
All inputs are finite; a program needn't handle non-finite values.
Results may differ from a plain program's by a relative error of at most 0.0069.
Values may be sent and summed in bfloat16 or wider, within the bound.
A program may use at most 192 MiB of HBM per device.

v0:
```python
import jax
import jax.numpy as jnp
from jax import lax
from jax.sharding import PartitionSpec as P

HALVES = 2


EPS = 1e-06
ROUTE_SCALE = 2.5


def partner(shard, axis, bit):
    return lax.ppermute(shard, axis, [(i, i ^ 1 << bit) for i in range(lax.axis_size(axis))])


def passed_along(block, axis, distance):
    devices = range(lax.axis_size(axis))
    route = [((i - distance) % len(devices), i) for i in devices]
    return lax.ppermute(block, axis, route)


def normalize(acts, gain):
    wide = acts.astype(jnp.float32)
    inverse = lax.rsqrt(jnp.mean(wide * wide, axis=-1, keepdims=True) + EPS)
    return (wide, inverse, (wide * inverse * gain).astype(jnp.bfloat16))


def gating(normed, table, choose):
    logits = jnp.dot(normed, table, preferred_element_type=jnp.float32)
    affinity = jax.nn.sigmoid(logits)
    onehot = (
        choose[:, :, None] == jnp.arange(table.shape[1], dtype=jnp.int32)[None, None, :]
    ).astype(jnp.float32)
    picked = jnp.sum(onehot * affinity[:, None, :], axis=2)
    total = jnp.sum(picked, axis=1, keepdims=True)
    return (onehot, picked, total, ROUTE_SCALE * picked / total)


def slot_of(choose, experts):
    flat = choose.reshape(-1)
    onehot = (flat[:, None] == jnp.arange(experts, dtype=jnp.int32)[None, :]).astype(jnp.int32)
    before = jnp.cumsum(onehot, axis=0) - onehot
    return jnp.sum(before * onehot, axis=1)


def dispatch_rows(rows, owner, where, count):
    fill = jnp.full((count,), rows.shape[0], jnp.int32).at[where].set(owner)
    padded = jnp.concatenate([rows, jnp.zeros((1, rows.shape[1]), rows.dtype)], axis=0)
    return jnp.take(padded, fill, axis=0)


def expert_forward(rows, up, down):
    pre = jnp.dot(rows, up, preferred_element_type=jnp.float32)
    hidden = jax.nn.silu(pre).astype(jnp.bfloat16)
    return jnp.dot(hidden, down, preferred_element_type=jnp.float32).astype(jnp.bfloat16)


def expert_backward(rows, grads, up, down):
    pre = jnp.dot(rows, up, preferred_element_type=jnp.float32)
    sigma = jax.nn.sigmoid(pre)
    hidden = (pre * sigma).astype(jnp.bfloat16)
    output = jnp.dot(hidden, down, preferred_element_type=jnp.float32).astype(jnp.bfloat16)
    back = lax.dot_general(
        grads, down, (((1,), (1,)), ((), ())), preferred_element_type=jnp.float32
    )
    dpre = (back * sigma * (1.0 + pre * (1.0 - sigma))).astype(jnp.bfloat16)
    dinput = lax.dot_general(dpre, up, (((1,), (1,)), ((), ())), preferred_element_type=jnp.float32)
    return (output, dinput.astype(jnp.bfloat16))


def router_grad(grads, routed, onehot, picked, total, table):
    dgate = jnp.sum(routed.astype(jnp.float32) * grads.astype(jnp.float32)[:, None, :], axis=2)
    dsel = ROUTE_SCALE / total * (dgate - jnp.sum(dgate * picked, axis=1, keepdims=True) / total)
    dlogit = jnp.sum(onehot * (dsel * picked * (1.0 - picked))[:, :, None], axis=1)
    return jnp.dot(dlogit, table.astype(jnp.float32).T, precision=lax.Precision.HIGHEST)


def norm_grad(grads, dnormed, wide, inverse, gain):
    scaled = dnormed * gain
    inner = jnp.mean(scaled * wide, axis=-1, keepdims=True)
    return (grads.astype(jnp.float32) + inverse * scaled - wide * inverse**3 * inner).astype(
        jnp.bfloat16
    )


def add_halves(first, second):
    return (first.astype(jnp.float32) + second.astype(jnp.float32)).astype(jnp.bfloat16)


def on_device(
    fwd_acts, bwd_saved, bwd_grads, norm_gain, router, w_up, w_down, fwd_experts, bwd_experts
):
    gain = norm_gain[0]
    table = router[0]
    up = w_up[0]
    down = w_down[0]
    tok_rows = fwd_acts.shape[1]
    width = fwd_acts.shape[2]
    experts = table.shape[1]
    top = fwd_experts.shape[2]
    capacity = 9 * tok_rows * top // (8 * experts)
    half_cap = capacity // HALVES
    devices = lax.axis_size("expert")
    count = tok_rows * top
    owner = jnp.arange(count, dtype=jnp.int32) // top
    every = jnp.arange(count, dtype=jnp.int32)
    room = experts * capacity
    choose_a = fwd_experts[0]
    wide_a, inv_a, normed_a = normalize(fwd_acts[0], gain)
    onehot_a, picked_a, total_a, gate_a = gating(normed_a, table, choose_a)
    where_a = choose_a.reshape(-1) * capacity + slot_of(choose_a, experts)
    buffer_a = dispatch_rows(normed_a, owner, where_a, room).reshape(experts, capacity, width)
    choose_b = bwd_experts[0]
    grads_b = bwd_grads[0]
    wide_b, inv_b, normed_b = normalize(bwd_saved[0], gain)
    onehot_b, picked_b, total_b, gate_b = gating(normed_b, table, choose_b)
    where_b = choose_b.reshape(-1) * capacity + slot_of(choose_b, experts)
    scaled_b = (
        (gate_b[:, :, None] * grads_b.astype(jnp.float32)[:, None, :])
        .astype(jnp.bfloat16)
        .reshape(count, width)
    )
    buffer_b = dispatch_rows(normed_b, owner, where_b, room).reshape(experts, capacity, width)
    grad_buf_b = dispatch_rows(scaled_b, every, where_b, room).reshape(experts, capacity, width)
    own_a = buffer_a.reshape(devices, half_cap, width)
    own_x = buffer_b.reshape(devices, half_cap, width)
    own_g = grad_buf_b.reshape(devices, half_cap, width)
    got_a = lax.all_to_all(own_a, "expert", split_axis=0, concat_axis=0, tiled=True)
    mate_a = partner(got_a, "expert", 0)
    part_a = expert_forward(jnp.stack([got_a, mate_a]).reshape(-1, width), up, down).reshape(
        HALVES, devices, half_cap, width
    )
    mine_a = partner(part_a[1], "expert", 0)
    back = lax.all_to_all(
        add_halves(part_a[0], mine_a), "expert", split_axis=0, concat_axis=0, tiled=True
    )
    got_x, got_g = (
        lax.all_to_all(own_x, "expert", split_axis=0, concat_axis=0, tiled=True),
        lax.all_to_all(own_g, "expert", split_axis=0, concat_axis=0, tiled=True),
    )
    mate_b = partner(jnp.stack([got_x, got_g]), "expert", 0)
    output, dinput = expert_backward(
        jnp.stack([got_x, mate_b[0]]).reshape(-1, width),
        jnp.stack([got_g, mate_b[1]]).reshape(-1, width),
        up,
        down,
    )
    output = output.reshape(HALVES, devices, half_cap, width)
    dinput = dinput.reshape(HALVES, devices, half_cap, width)
    mine_b = partner(jnp.stack([output[1], dinput[1]]), "expert", 0)
    back_out, back_in = (
        lax.all_to_all(
            add_halves(output[0], mine_b[0]), "expert", split_axis=0, concat_axis=0, tiled=True
        ),
        lax.all_to_all(
            add_halves(dinput[0], mine_b[1]), "expert", split_axis=0, concat_axis=0, tiled=True
        ),
    )
    result_a = back.reshape(experts, capacity, width)
    result_b = back_out.reshape(experts, capacity, width)
    dresult_b = back_in.reshape(experts, capacity, width)
    routed_a = jnp.take(result_a.reshape(-1, width), where_a, axis=0).reshape(tok_rows, top, width)
    moe_a = jnp.sum(gate_a[:, :, None] * routed_a.astype(jnp.float32), axis=1)
    out_a = (wide_a + moe_a).astype(jnp.bfloat16)
    routed_b = jnp.take(result_b.reshape(-1, width), where_b, axis=0).reshape(tok_rows, top, width)
    droutes_b = jnp.take(dresult_b.reshape(-1, width), where_b, axis=0).reshape(
        tok_rows, top, width
    )
    dnormed = jnp.sum(droutes_b.astype(jnp.float32), axis=1) + router_grad(
        grads_b, routed_b, onehot_b, picked_b, total_b, table
    )
    dx_b = norm_grad(grads_b, dnormed, wide_b, inv_b, gain)
    fwd_next = passed_along(out_a[None], "pipe", 1)
    bwd_next = passed_along(dx_b[None], "pipe", -1)
    return (fwd_next, bwd_next)


def solution(mesh):
    placed = (
        P("pipe", "expert", None),
        P("pipe", "expert", None),
        P("pipe", "expert", None),
        P("pipe", None),
        P("pipe", None, None),
        P("pipe", None, "expert"),
        P("pipe", "expert", None),
        P("pipe", "expert", None),
        P("pipe", "expert", None),
    )
    return jax.shard_map(
        on_device,
        mesh=mesh,
        in_specs=placed,
        out_specs=(P("pipe", "expert", None), P("pipe", "expert", None)),
        check_vma=False,
    )
```

profile of v0, /device:TPU:0, one launch (start us, length us, event | category | flops | bytes accessed | tf_op | source)
XLA Modules:
  0.0 544.4 jit_solution(2628435843455924093)
XLA Ops:
  13.3 5.6 %mul.271 = f32[256,3584]{1,0:T(8,128)} reshape(f32[128,2,3584]{2,1,0:T(2,128)} %mul.270) | data formatting | bytes 7340032 | tf_op jit(solution)/shard_map/mul | solution.py:120
  29.4 6.5 %all-to-all-start.2 = ((bf16[8,36,3584]{2,1,0:T(8,128)(2,1)}), bf16[8,36,3584]{2,1,0:T(8,128)(2,1)S(1)}, u32[]{:S(2)}, u32[]{:S(2)}) async-start(bf16[8,36,3584]{2,1,0:T(8,128)(2,1)} %broadcast_select_fusion), calls=%async_computation.2 | async-start | bytes 4587520 | tf_op jit(solution)/shard_map/all_to_all | solution.py:140
  53.0 36.1 %all-to-all-done.2 = bf16[8,36,3584]{2,1,0:T(8,128)(2,1)S(1)} async-done(((bf16[8,36,3584]{2,1,0:T(8,128)(2,1)}), bf16[8,36,3584]{2,1,0:T(8,128)(2,1)S(1)}, u32[]{:S(2)}, u32[]{:S(2)}) %all-to-all-start.2) | async-done | bytes 2064416 | tf_op jit(solution)/shard_map/all_to_all | solution.py:140
  107.3 39.8 %all-to-all-done = bf16[8,36,3584]{2,1,0:T(8,128)(2,1)} async-done(((bf16[8,36,3584]{2,1,0:T(8,128)(2,1)}), bf16[8,36,3584]{2,1,0:T(8,128)(2,1)}, u32[]{:S(2)}, u32[]{:S(2)}) %all-to-all-start) | async-done | bytes 2064416 | tf_op jit(solution)/shard_map/all_to_all | solution.py:129
  155.4 49.3 %all-to-all-done.3 = bf16[8,36,3584]{2,1,0:T(8,128)(2,1)} async-done(((bf16[8,36,3584]{2,1,0:T(8,128)(2,1)}), bf16[8,36,3584]{2,1,0:T(8,128)(2,1)}, u32[]{:S(2)}, u32[]{:S(2)}) %all-to-all-start.3) | async-done | bytes 2064416 | tf_op jit(solution)/shard_map/all_to_all | solution.py:139
  216.2 7.0 %reshape.320 = bf16[576,3584]{1,0:T(8,128)(2,1)} reshape(bf16[2,8,36,3584]{3,2,1,0:T(8,128)(2,1)} %pad_maximum_fusion.2) | data formatting | bytes 8257536 | tf_op jit(solution)/shard_map/reshape | solution.py:131
  223.2 5.9 %multiply_convert_fusion.2 = bf16[576,512]{1,0:T(8,128)(2,1)S(1)} fusion(bf16[576,3584]{1,0:T(8,128)(2,1)} %reshape.320, bf16[1,3584,512]{2,1,0:T(8,128)(2,1)} %param.18), kind=kOutput, calls=%fused_computation.78 | convolution fusion | flops 2115403776 | bytes 8388608 | tf_op jit(solution)/shard_map/dot_general | solution.py:54
  249.5 7.1 %reshape.322 = bf16[576,3584]{1,0:T(8,128)(2,1)} reshape(bf16[2,8,36,3584]{3,2,1,0:T(8,128)(2,1)} %pad_maximum_fusion.3) | data formatting | bytes 8257536 | tf_op jit(solution)/shard_map/reshape | solution.py:145
  261.4 15.3 %reshape.323 = bf16[576,3584]{1,0:T(8,128)(2,1)} reshape(bf16[2,8,36,3584]{3,2,1,0:T(8,128)(2,1)} %pad_maximum_fusion) | data formatting | bytes 8257536 | tf_op jit(solution)/shard_map/reshape | solution.py:144
  276.6 5.7 %fusion.8 = f32[576,512]{1,0:T(8,128)S(1)} fusion(bf16[576,3584]{1,0:T(8,128)(2,1)} %reshape.323, bf16[1,3584,512]{2,1,0:T(8,128)(2,1)} %param.18), kind=kOutput, calls=%fused_computation.29 | convolution fusion | flops 2113929216 | bytes 8978432 | tf_op jit(solution)/shard_map/dot_general | solution.py:60
  297.2 5.2 slice_convert_fusion
  311.6 4.8 reshape.325
  316.5 5.3 add_convert_fusion
  325.4 4.9 reshape.332
  336.4 42.2 %all-to-all-done.1 = bf16[8,36,3584]{2,1,0:T(8,128)(2,1)S(1)} async-done(((bf16[8,36,3584]{2,1,0:T(8,128)(2,1)}), bf16[8,36,3584]{2,1,0:T(8,128)(2,1)S(1)}, u32[]{:S(2)}, u32[]{:S(2)}) %all-to-all-start.1) | async-done | bytes 2064416 | tf_op jit(solution)/shard_map/all_to_all | solution.py:135
  385.1 5.0 reshape.329
  390.1 4.8 fusion.2
  394.9 43.0 %all-to-all-done.5 = bf16[8,36,3584]{2,1,0:T(8,128)(2,1)} async-done(((bf16[8,36,3584]{2,1,0:T(8,128)(2,1)}), bf16[8,36,3584]{2,1,0:T(8,128)(2,1)}, u32[]{:S(2)}, u32[]{:S(2)}) %all-to-all-start.5) | async-done | bytes 2064416 | tf_op jit(solution)/shard_map/all_to_all | solution.py:153
  451.6 5.6 %reshape.326 = f32[128,2,3584]{2,1,0:T(2,128)} reshape(f32[256,3584]{1,0:T(8,128)} %select_convert_fusion.1) | data formatting | bytes 7340032 | tf_op jit(solution)/shard_map/convert_element_type | solution.py:164
  457.1 7.2 %multiply_reduce_fusion.1 = f32[128,3584]{1,0:T(8,128)S(1)} fusion(f32[128,2,3584]{2,1,0:T(2,128)} %reshape.326, f32[128,2]{1,0:T(8,128)S(1)} %copy.57), kind=kLoop, calls=%fused_computation.35 | loop fusion | flops 1376256 | bytes 5506048 | tf_op jit(solution)/shard_map/reduce_sum | solution.py:164
  476.3 19.2 %all-to-all-done.4 = bf16[8,36,3584]{2,1,0:T(8,128)(2,1)} async-done(((bf16[8,36,3584]{2,1,0:T(8,128)(2,1)}), bf16[8,36,3584]{2,1,0:T(8,128)(2,1)}, u32[]{:S(2)}, u32[]{:S(2)}) %all-to-all-start.4) | async-done | bytes 2064416 | tf_op jit(solution)/shard_map/all_to_all | solution.py:156
  504.7 5.6 %reshape.331 = f32[128,2,3584]{2,1,0:T(2,128)} reshape(f32[256,3584]{1,0:T(8,128)} %select_convert_fusion) | data formatting | bytes 7340032 | tf_op jit(solution)/shard_map/convert_element_type | solution.py:170
  510.2 6.6 %reduce_sum.146 = f32[128,3584]{1,0:T(8,128)S(1)} reduce(f32[128,2,3584]{2,1,0:T(2,128)} %reshape.331, f32[]{:T(128)} %constant.53.clone.1), dimensions={1}, to_apply=%region_16.19 | reduce | flops 458752 | bytes 5505028 | tf_op jit(solution)/shard_map/reduce_sum | solution.py:170
  521.5 19.4 %collective-permute-done.5 = bf16[1,128,3584]{2,1,0:T(8,128)(2,1)S(1)} collective-permute-done((bf16[1,128,3584]{2,1,0:T(8,128)(2,1)S(1)}, bf16[1,128,3584]{2,1,0:T(8,128)(2,1)S(1)}, u32[]{:S(2)}, u32[]{:S(2)}) %collective-permute-start.5) | collective-permute-done | bytes 917536 | tf_op jit(solution)/shard_map/ppermute | solution.py:20
  (187 shorter events, 185.9 us)
Async XLA Ops:
  0.6 8.7 %copy-start = (bf16[1,3584,4]{1,2,0:T(4,128)(2,1)S(1)}, bf16[1,3584,4]{1,2,0:T(4,128)(2,1)}, u32[]{:S(2)}) copy-start(bf16[1,3584,4]{1,2,0:T(4,128)(2,1)} %param.17) | copy-start | bytes 86020
  0.6 9.1 %copy-start.11 = (s32[1,128,2]{1,2,0:T(2,128)S(1)}, s32[1,128,2]{1,2,0:T(2,128)}, u32[]{:S(2)}) copy-start(s32[1,128,2]{1,2,0:T(2,128)} %param.21) | copy-start | bytes 3076
  0.7 8.7 %copy-start.2 = (bf16[1,128,3584]{2,1,0:T(8,128)(2,1)S(1)}, bf16[1,128,3584]{2,1,0:T(8,128)(2,1)}, u32[]{:S(2)}) copy-start(bf16[1,128,3584]{2,1,0:T(8,128)(2,1)} %param.14) | copy-start | bytes 2752516
  0.7 8.6 %copy-start.15 = (f32[1,3584]{1,0:T(1,128)S(1)}, f32[1,3584]{1,0:T(1,128)}, u32[]{:S(2)}) copy-start(f32[1,3584]{1,0:T(1,128)} %param.16) | copy-start | bytes 43012
  1.6 8.5 %copy-start.9 = (bf16[1,128,3584]{2,1,0:T(8,128)(2,1)S(1)}, bf16[1,128,3584]{2,1,0:T(8,128)(2,1)}, u32[]{:S(2)}) copy-start(bf16[1,128,3584]{2,1,0:T(8,128)(2,1)} %param.15) | copy-start | bytes 2752516
  29.4 6.5 %copy-start.16 = (s32[1,128,2]{1,2,0:T(2,128)S(1)}, s32[1,128,2]{1,2,0:T(2,128)}, u32[]{:S(2)}) copy-start(s32[1,128,2]{1,2,0:T(2,128)} %param.20) | copy-start | bytes 3076
  29.4 59.7 %all-to-all-start.2 = ((bf16[8,36,3584]{2,1,0:T(8,128)(2,1)}), bf16[8,36,3584]{2,1,0:T(8,128)(2,1)S(1)}, u32[]{:S(2)}, u32[]{:S(2)}) async-start(bf16[8,36,3584]{2,1,0:T(8,128)(2,1)} %broadcast_select_fusion), calls=%async_computation.2 | async-start | bytes 4587520 | tf_op jit(solution)/shard_map/all_to_all | solution.py:140
  89.1 57.9 %all-to-all-start = ((bf16[8,36,3584]{2,1,0:T(8,128)(2,1)}), bf16[8,36,3584]{2,1,0:T(8,128)(2,1)}, u32[]{:S(2)}, u32[]{:S(2)}) async-start(bf16[8,36,3584]{2,1,0:T(8,128)(2,1)} %reshape_reshape.16), calls=%async_computation | async-start | bytes 4587520 | tf_op jit(solution)/shard_map/all_to_all | solution.py:129
  147.0 57.6 %all-to-all-start.3 = ((bf16[8,36,3584]{2,1,0:T(8,128)(2,1)}), bf16[8,36,3584]{2,1,0:T(8,128)(2,1)}, u32[]{:S(2)}, u32[]{:S(2)}) async-start(bf16[8,36,3584]{2,1,0:T(8,128)(2,1)} %reshape_reshape.18), calls=%async_computation.3 | async-start | bytes 4587520 | tf_op jit(solution)/shard_map/all_to_all | solution.py:139
  155.0 54.9 %collective-permute-start = (bf16[8,36,3584]{2,0,1:T(8,128)(2,1)}, bf16[8,36,3584]{2,0,1:T(8,128)(2,1)}, u32[]{:S(2)}, u32[]{:S(2)}) collective-permute-start(bf16[8,36,3584]{2,0,1:T(8,128)(2,1)} %copy.63), channel_id=1, source_target_pairs={{0,1},{1,0},{2,3},{3,2},{4,5},{5,4},{6,7},{7,6},{8,9},{9,8},{10,11... | collective-permute-start | bytes 6193160 | tf_op jit(solution)/shard_map/ppermute | solution.py:14
  209.9 32.7 %collective-permute-start.3 = (bf16[2,8,36,3584]{3,1,2,0:T(8,128)(2,1)}, bf16[2,8,36,3584]{3,1,2,0:T(8,128)(2,1)}, u32[]{:S(2)}, u32[]{:S(2)}) collective-permute-start(bf16[2,8,36,3584]{3,1,2,0:T(8,128)(2,1)} %copy.73), channel_id=1, source_target_pairs={{0,1},{1,0},{2,3},{3,2},{4,5},{5,4},{6,7},{7,6},{8,9},{9,8},{10,11... | collective-permute-start | bytes 12386312 | tf_op jit(solution)/shard_map/ppermute | solution.py:14
  223.2 5.9 %copy-start.20 = (bf16[1,512,3584]{2,1,0:T(8,128)(2,1)S(1)}, bf16[1,512,3584]{2,1,0:T(8,128)(2,1)}, u32[]{:S(2)}) copy-start(bf16[1,512,3584]{2,1,0:T(8,128)(2,1)} %param.19) | copy-start | bytes 11010052
  242.1 74.4 %collective-permute-start.1 = (bf16[8,36,3584]{2,0,1:T(8,128)(2,1)}, bf16[8,36,3584]{2,0,1:T(8,128)(2,1)}, u32[]{:S(2)}, u32[]{:S(2)}) collective-permute-start(bf16[8,36,3584]{2,0,1:T(8,128)(2,1)} %copy.65), channel_id=1, source_target_pairs={{0,1},{1,0},{2,3},{3,2},{4,5},{5,4},{6,7},{7,6},{8,9},{9,8},{10,11... | collective-permute-start | bytes 6193160 | tf_op jit(solution)/shard_map/ppermute | solution.py:14
  249.5 7.1 %copy-start.6 = (bf16[1,8,36,3584]{3,1,2,0:T(8,128)(2,1)S(1)}, bf16[1,8,36,3584]{3,1,2,0:T(8,128)(2,1)}, u32[]{:S(2)}) copy-start(bf16[1,8,36,3584]{3,1,2,0:T(8,128)(2,1)} %get-tuple-element.18) | copy-start | bytes 6193156
  276.6 5.7 %copy-start.21 = (bf16[1,512,3584]{2,1,0:T(8,128)(2,1)S(1)}, bf16[1,512,3584]{2,1,0:T(8,128)(2,1)}, u32[]{:S(2)}) copy-start(bf16[1,512,3584]{2,1,0:T(8,128)(2,1)} %param.19) | copy-start | bytes 11010052
  311.6 18.6 %collective-permute-start.4 = (bf16[2,8,36,3584]{3,1,2,0:T(8,128)(2,1)}, bf16[2,8,36,3584]{3,1,2,0:T(8,128)(2,1)}, u32[]{:S(2)}, u32[]{:S(2)}) collective-permute-start(bf16[2,8,36,3584]{3,1,2,0:T(8,128)(2,1)} %copy.76), channel_id=1, source_target_pairs={{0,1},{1,0},{2,3},{3,2},{4,5},{5,4},{6,7},{7,6},{8,9},{9,8},{10,11... | collective-permute-start | bytes 12386312 | tf_op jit(solution)/shard_map/ppermute | solution.py:14
  321.8 56.8 %all-to-all-start.1 = ((bf16[8,36,3584]{2,1,0:T(8,128)(2,1)}), bf16[8,36,3584]{2,1,0:T(8,128)(2,1)S(1)}, u32[]{:S(2)}, u32[]{:S(2)}) async-start(bf16[8,36,3584]{2,1,0:T(8,128)(2,1)} %add_convert_fusion), calls=%async_computation.1 | async-start | bytes 4587520 | tf_op jit(solution)/shard_map/all_to_all | solution.py:135
  336.4 48.2 %copy-start.7 = (bf16[1,128,3584]{2,1,0:T(8,128)(2,1)S(1)}, bf16[1,128,3584]{2,1,0:T(8,128)(2,1)}, u32[]{:S(2)}) copy-start(bf16[1,128,3584]{2,1,0:T(8,128)(2,1)} %param.13) | copy-start | bytes 2752516
  380.0 57.9 %all-to-all-start.5 = ((bf16[8,36,3584]{2,1,0:T(8,128)(2,1)}), bf16[8,36,3584]{2,1,0:T(8,128)(2,1)}, u32[]{:S(2)}, u32[]{:S(2)}) async-start(bf16[8,36,3584]{2,1,0:T(8,128)(2,1)} %fusion.1), calls=%async_computation.5 | async-start | bytes 4587520 | tf_op jit(solution)/shard_map/all_to_all | solution.py:153
  385.1 5.0 copy-start.5
  437.9 57.7 %all-to-all-start.4 = ((bf16[8,36,3584]{2,1,0:T(8,128)(2,1)}), bf16[8,36,3584]{2,1,0:T(8,128)(2,1)}, u32[]{:S(2)}, u32[]{:S(2)}) async-start(bf16[8,36,3584]{2,1,0:T(8,128)(2,1)} %fusion.2), calls=%async_computation.4 | async-start | bytes 4587520 | tf_op jit(solution)/shard_map/all_to_all | solution.py:156
  465.4 56.0 %collective-permute-start.2 = (bf16[1,128,3584]{2,1,0:T(8,128)(2,1)}, bf16[1,128,3584]{2,1,0:T(8,128)(2,1)}, u32[]{:S(2)}, u32[]{:S(2)}) collective-permute-start(bf16[1,128,3584]{2,1,0:T(8,128)(2,1)} %fusion.32), channel_id=1, source_target_pairs={{24,0},{0,8},{8,16},{16,24},{25,1},{1,9},{9,17},{17,25},{26,2},{2,... | collective-permute-start | bytes 2752520 | tf_op jit(solution)/shard_map/ppermute | solution.py:20
  510.2 6.6 %copy-start.3 = (bf16[1,128,3584]{2,1,0:T(8,128)(2,1)S(1)}, bf16[1,128,3584]{2,1,0:T(8,128)(2,1)}, u32[]{:S(2)}) copy-start(bf16[1,128,3584]{2,1,0:T(8,128)(2,1)} %param.14) | copy-start | bytes 2752516
  519.0 21.9 %collective-permute-start.5 = (bf16[1,128,3584]{2,1,0:T(8,128)(2,1)S(1)}, bf16[1,128,3584]{2,1,0:T(8,128)(2,1)S(1)}, u32[]{:S(2)}, u32[]{:S(2)}) collective-permute-start(bf16[1,128,3584]{2,1,0:T(8,128)(2,1)S(1)} %fusion.54), channel_id=1, source_target_pairs={{8,0},{16,8},{24,16},{0,24},{9,1},{17,9},{25,17},{1,25},{10,2},{18... | collective-permute-start | bytes 2752520 | tf_op jit(solution)/shard_map/ppermute | solution.py:20
  (11 other events, 32.5 us)
where the time goes:
time: 555 us; the launch traced here: 544 us
  waiting for transfers between devices  249 us (45%)
  local copies, waits for them, and re-layouts  150 us (27%)
  other arithmetic  85.1 us (15%)
  starting transfers between devices  32.9 us (6%)
  matrix products  25.2 us (5%)
    all_to_all x1, waiting for transfers between devices, on_device(): lax.all_to_all(own_x, 'expert', split_axis=0, concat_axis=0, tiled=True)  49.3 us
    all_to_all x1, waiting for transfers between devices, on_device(): lax.all_to_all(add_halves(output[0], mine_b[0]), 'expert', split_axis=0,...  43 us
    all_to_all x1, waiting for transfers between devices, on_device(): lax.all_to_all(add_halves(part_a[0], mine_a), 'expert', split_axis=0, con...  42.2 us
    all_to_all x1, waiting for transfers between devices, on_device(): lax.all_to_all(own_a, 'expert', split_axis=0, concat_axis=0, tiled=True)  39.8 us
    all_to_all x1, waiting for transfers between devices, on_device(): lax.all_to_all(own_g, 'expert', split_axis=0, concat_axis=0, tiled=True)  36.1 us
    ppermute x2, waiting for transfers between devices, passed_along(): return lax.ppermute(block, axis, route)  19.4 us
    all_to_all x1, waiting for transfers between devices, on_device(): lax.all_to_all(add_halves(dinput[0], mine_b[1]), 'expert', split_axis=0,...  19.2 us
    reshape x1, local copies, waits for them, and re-layouts, on_device(): jnp.stack([got_x, mate_b[0]]).reshape(-1, width)  15.3 us
  transfers between devices with their start and end apart: 12, of which 7 were waited for; matrix products, arithmetic and copies ran while one was open for 42% of the time, Pallas kernels for 0%

commit v1 on v0

v1 whole, which is shorter than its diff:
```python
import jax
import jax.numpy as jnp
from jax import lax
from jax.sharding import PartitionSpec as P

HALVES = 2
EPS = 1e-06
ROUTE_SCALE = 2.5


def partner(shard, axis, bit):
    return lax.ppermute(shard, axis, [(i, i ^ 1 << bit) for i in range(lax.axis_size(axis))])


def passed_along(block, axis, distance):
    devices = range(lax.axis_size(axis))
    route = [((i - distance) % len(devices), i) for i in devices]
    return lax.ppermute(block, axis, route)


def normalize(acts, gain):
    wide = acts.astype(jnp.float32)
    inverse = lax.rsqrt(jnp.mean(wide * wide, axis=-1, keepdims=True) + EPS)
    return (wide, inverse, (wide * inverse * gain).astype(jnp.bfloat16))


def gating(normed, table, choose):
    logits = jnp.dot(normed, table, preferred_element_type=jnp.float32)
    affinity = jax.nn.sigmoid(logits)
    onehot = (
        choose[:, :, None] == jnp.arange(table.shape[1], dtype=jnp.int32)[None, None, :]
    ).astype(jnp.float32)
    picked = jnp.sum(onehot * affinity[:, None, :], axis=2)
    total = jnp.sum(picked, axis=1, keepdims=True)
    return (onehot, picked, total, ROUTE_SCALE * picked / total)


def slot_masks(choose, experts, capacity):
    tok_rows, top = choose.shape
    flat = choose.reshape(-1)
    count = tok_rows * top
    onehot = (flat[:, None] == jnp.arange(experts, dtype=jnp.int32)[None, :]).astype(jnp.bfloat16)
    at = jnp.arange(count, dtype=jnp.int32)
    earlier = (at[None, :] < at[:, None]).astype(jnp.bfloat16)
    before = jnp.dot(earlier, onehot, preferred_element_type=jnp.float32)
    slot = jnp.sum(before * onehot.astype(jnp.float32), axis=1).astype(jnp.int32)
    where = (flat * capacity + slot).reshape(tok_rows, top)
    places = jnp.arange(experts * capacity, dtype=jnp.int32)
    return [(places[:, None] == where[None, :, k]).astype(jnp.bfloat16) for k in range(top)]


def pick(mask, rows):
    return jnp.dot(mask, rows, preferred_element_type=jnp.float32).astype(jnp.bfloat16)


def back_to_tokens(mask, rows):
    return lax.dot_general(
        mask, rows, (((0,), (0,)), ((), ())), preferred_element_type=jnp.float32
    )


def swap(rows):
    return lax.all_to_all(rows, "expert", split_axis=0, concat_axis=0, tiled=True)


def on_device(
    fwd_acts, bwd_saved, bwd_grads, norm_gain, router, w_up, w_down, fwd_experts, bwd_experts
):
    gain = norm_gain[0]
    table = router[0]
    width = fwd_acts.shape[2]
    tok_rows = fwd_acts.shape[1]
    experts = table.shape[1]
    top = fwd_experts.shape[2]
    capacity = 9 * tok_rows * top // (8 * experts)
    half_cap = capacity // HALVES
    devices = lax.axis_size("expert")
    shape = (devices, half_cap, width)
    ups = [w_up[0], partner(w_up[0], "expert", 0)]
    downs = [w_down[0], partner(w_down[0], "expert", 0)]

    choose_a = fwd_experts[0]
    masks_a = slot_masks(choose_a, experts, capacity)
    wide_a, inv_a, normed_a = normalize(fwd_acts[0], gain)
    got_a = swap(pick(sum(masks_a), normed_a).reshape(shape)).reshape(-1, width)
    _, _, _, gate_a = gating(normed_a, table, choose_a)

    choose_b = bwd_experts[0]
    grads_b = bwd_grads[0]
    masks_b = slot_masks(choose_b, experts, capacity)
    wide_b, inv_b, normed_b = normalize(bwd_saved[0], gain)
    spread = sum(masks_b)
    got_x = swap(pick(spread, normed_b).reshape(shape)).reshape(-1, width)
    got_g = swap(pick(spread, grads_b).reshape(shape)).reshape(-1, width)
    onehot_b, picked_b, total_b, gate_b = gating(normed_b, table, choose_b)

    y = jnp.zeros((devices * half_cap, width), jnp.float32)
    for up, down in zip(ups, downs):
        hidden = jax.nn.silu(jnp.dot(got_a, up, preferred_element_type=jnp.float32))
        y += jnp.dot(hidden.astype(jnp.bfloat16), down, preferred_element_type=jnp.float32)
    back_a = swap(y.astype(jnp.bfloat16).reshape(shape)).reshape(-1, width)

    dx = jnp.zeros((devices * half_cap, width), jnp.float32)
    dgate_rows = jnp.zeros((devices * half_cap,), jnp.float32)
    for up, down in zip(ups, downs):
        pre = jnp.dot(got_x, up, preferred_element_type=jnp.float32)
        sigma = jax.nn.sigmoid(pre)
        hidden = (pre * sigma).astype(jnp.bfloat16).astype(jnp.float32)
        back = lax.dot_general(
            got_g, down, (((1,), (1,)), ((), ())), preferred_element_type=jnp.float32
        )
        dgate_rows += jnp.sum(hidden * back, axis=1)
        dpre = (back * sigma * (1.0 + pre * (1.0 - sigma))).astype(jnp.bfloat16)
        dx += lax.dot_general(dpre, up, (((1,), (1,)), ((), ())), preferred_element_type=jnp.float32)
    back_g = swap(dgate_rows.reshape(devices, half_cap)).reshape(-1)
    back_x = swap(dx.astype(jnp.bfloat16).reshape(shape)).reshape(-1, width)

    out_a = wide_a
    for k in range(top):
        out_a = out_a + gate_a[:, k : k + 1] * back_to_tokens(masks_a[k], back_a)
    fwd_next = passed_along(out_a.astype(jnp.bfloat16)[None], "pipe", 1)

    dgate = jnp.stack(
        [jnp.sum(m.astype(jnp.float32) * back_g[:, None], axis=0) for m in masks_b], axis=1
    )
    dsel = ROUTE_SCALE / total_b * (
        dgate - jnp.sum(dgate * picked_b, axis=1, keepdims=True) / total_b
    )
    dlogit = jnp.sum(onehot_b * (dsel * picked_b * (1.0 - picked_b))[:, :, None], axis=1)
    dnormed = jnp.dot(dlogit, table.astype(jnp.float32).T, precision=lax.Precision.HIGHEST)
    for k in range(top):
        dnormed = dnormed + gate_b[:, k : k + 1] * back_to_tokens(masks_b[k], back_x)
    scaled = dnormed * gain
    inner = jnp.mean(scaled * wide_b, axis=-1, keepdims=True)
    dx_b = grads_b.astype(jnp.float32) + inv_b * scaled - wide_b * inv_b**3 * inner
    bwd_next = passed_along(dx_b.astype(jnp.bfloat16)[None], "pipe", -1)
    return (fwd_next, bwd_next)


def solution(mesh):
    placed = (
        P("pipe", "expert", None),
        P("pipe", "expert", None),
        P("pipe", "expert", None),
        P("pipe", None),
        P("pipe", None, None),
        P("pipe", None, "expert"),
        P("pipe", "expert", None),
        P("pipe", "expert", None),
        P("pipe", "expert", None),
    )
    return jax.shard_map(
        on_device,
        mesh=mesh,
        in_specs=placed,
        out_specs=(P("pipe", "expert", None), P("pipe", "expert", None)),
        check_vma=False,
    )
```

time: 555 us -> 372 us (0.67)
  the two profiles are of different devices: /device:TPU:0 before, /device:TPU:10 now
where the time goes in v1:
time: 372 us; the launch traced here: 367 us
  waiting for transfers between devices  234 us (63%)
  matrix products  50.8 us (14%)
  starting transfers between devices  42.8 us (12%)
  local copies, waits for them, and re-layouts  34.8 us (9%)
  other arithmetic  4.27 us (1%)
    all_to_all x6, waiting for transfers between devices, swap(): lax.all_to_all(rows, 'expert', split_axis=0, concat_axis=0, tiled=True)  211 us
    all_to_all x6, starting transfers between devices, swap(): lax.all_to_all(rows, 'expert', split_axis=0, concat_axis=0, tiled=True)  40.2 us
    ppermute x2, waiting for transfers between devices, passed_along(): return lax.ppermute(block, axis, route)  22.7 us
    dot_general x2, matrix products, on_device(): jnp.dot(hidden.astype(jnp.bfloat16), down, preferred_element_type=jnp.flo...  15.7 us
    dot_general x2, matrix products, on_device(): pre = jnp.dot(got_x, up, preferred_element_type=jnp.float32)  8.05 us
  transfers between devices with their start and end apart: 10, of which 6 were waited for; matrix products, arithmetic and copies ran while one was open for 20% of the time, Pallas kernels for 0%

profile of v1, /device:TPU:10, one launch (start us, length us, event | category | flops | bytes accessed | tf_op | source)
XLA Modules:
  0.0 367.4 jit_solution(2979492236520246439)
XLA Ops:
  7.3 5.5 %all-to-all-start = ((bf16[8,36,3584]{2,1,0:T(8,128)(2,1)}), bf16[8,36,3584]{2,1,0:T(8,128)(2,1)}, u32[]{:S(2)}, u32[]{:S(2)}) async-start(bf16[8,36,3584]{2,1,0:T(8,128)(2,1)} %reshape.198), calls=%async_computation | async-start | bytes 4587520 | tf_op jit(solution)/shard_map/all_to_all | solution.py:63
  16.8 45.8 %all-to-all-done = bf16[8,36,3584]{2,1,0:T(8,128)(2,1)} async-done(((bf16[8,36,3584]{2,1,0:T(8,128)(2,1)}), bf16[8,36,3584]{2,1,0:T(8,128)(2,1)}, u32[]{:S(2)}, u32[]{:S(2)}) %all-to-all-start) | async-done | bytes 2064416 | tf_op jit(solution)/shard_map/all_to_all | solution.py:63
  62.6 7.8 %all-to-all-start.2 = ((bf16[8,36,3584]{2,1,0:T(8,128)(2,1)}), bf16[8,36,3584]{2,1,0:T(8,128)(2,1)}, u32[]{:S(2)}, u32[]{:S(2)}) async-start(bf16[8,36,3584]{2,1,0:T(8,128)(2,1)} %reshape.202), calls=%async_computation.2 | async-start | bytes 4587520 | tf_op jit(solution)/shard_map/all_to_all | solution.py:63
  74.4 45.8 %all-to-all-done.2 = bf16[8,36,3584]{2,1,0:T(8,128)(2,1)} async-done(((bf16[8,36,3584]{2,1,0:T(8,128)(2,1)}), bf16[8,36,3584]{2,1,0:T(8,128)(2,1)}, u32[]{:S(2)}, u32[]{:S(2)}) %all-to-all-start.2) | async-done | bytes 2064416 | tf_op jit(solution)/shard_map/all_to_all | solution.py:63
  120.2 7.1 %all-to-all-start.3 = ((bf16[8,36,3584]{2,1,0:T(8,128)(2,1)}), bf16[8,36,3584]{2,1,0:T(8,128)(2,1)S(1)}, u32[]{:S(2)}, u32[]{:S(2)}) async-start(bf16[8,36,3584]{2,1,0:T(8,128)(2,1)} %reshape.204), calls=%async_computation.3 | async-start | bytes 4587520 | tf_op jit(solution)/shard_map/all_to_all | solution.py:63
  127.9 4.0 %reshape.199 = bf16[288,3584]{1,0:T(8,128)(2,1)} reshape(bf16[8,36,3584]{2,1,0:T(8,128)(2,1)} %all-to-all-done) | data formatting | bytes 4128768 | tf_op jit(solution)/shard_map/reshape | solution.py:85
  131.9 4.0 %reshape.203 = bf16[288,3584]{1,0:T(8,128)(2,1)} reshape(bf16[8,36,3584]{2,1,0:T(8,128)(2,1)} %all-to-all-done.2) | data formatting | bytes 4128768 | tf_op jit(solution)/shard_map/reshape | solution.py:93
  135.9 41.3 %all-to-all-done.3 = bf16[8,36,3584]{2,1,0:T(8,128)(2,1)S(1)} async-done(((bf16[8,36,3584]{2,1,0:T(8,128)(2,1)}), bf16[8,36,3584]{2,1,0:T(8,128)(2,1)S(1)}, u32[]{:S(2)}, u32[]{:S(2)}) %all-to-all-start.3) | async-done | bytes 2064416 | tf_op jit(solution)/shard_map/all_to_all | solution.py:63
  179.2 4.0 %fusion.91 = f32[288,512]{1,0:T(8,128)S(1)} fusion(bf16[288,3584]{1,0:T(8,128)(2,1)} %reshape.203, bf16[1,3584,512]{2,1,0:T(8,128)(2,1)} %param.14), kind=kOutput, calls=%fused_computation.146 | convolution fusion | flops 1056964608 | bytes 6324224 | tf_op jit(solution)/shard_map/dot_general | solution.py:106
  186.2 7.5 %fusion.53 = f32[288,3584]{1,0:T(8,128)} fusion(bf16[1,512,3584]{2,1,0:T(8,128)(2,1)} %param.15, bf16[288,3584]{1,0:T(8,128)(2,1)S(1)} %copy-done.5, bf16[1,3584,512]{2,1,0:T(8,128)(2,1)} %param.14), kind=kOutput, calls=%fused_computation.76 | convolution fusion | flops 2114666496 | bytes 13533184 | tf_op jit(solution)/shard_map/dot_general | solution.py:100
  193.7 4.0 %fusion.105 = f32[288,512]{1,0:T(8,128)S(1)} fusion(bf16[288,3584]{1,0:T(8,128)(2,1)} %reshape.203, bf16[3584,512]{1,0:T(8,128)(2,1)} %collective-permute-done), kind=kOutput, calls=%fused_computation.155 | convolution fusion | flops 1056964608 | bytes 6324224 | tf_op jit(solution)/shard_map/dot_general | solution.py:106
  197.8 4.3 %multiply_reduce_fusion = (f32[288]{0:T(512)S(1)}, f32[288,512]{1,0:T(8,128)}) fusion(f32[288,512]{1,0:T(8,128)S(1)} %fusion.105, bf16[288,3584]{1,0:T(8,128)(2,1)S(1)} %copy-done.7, bf16[512,3584]{1,0:T(8,128)(2,1)} %collective-permute-done.1), kind=kOutput, calls=%fused_computation.68 | convolution fusion | flops 1058144000 | bytes 6915200 | tf_op jit(solution)/shard_map/dot_general | solution.py:109
  202.8 6.7 %all-to-all-start.4 = ((f32[8,1,36]{2,1,0:T(1,128)}), f32[8,1,36]{2,1,0:T(1,128)S(1)}, u32[]{:S(2)}, u32[]{:S(2)}) async-start(f32[8,1,36]{2,1,0:T(1,128)} %add.109), calls=%async_computation.4 | async-start | bytes 8192 | tf_op jit(solution)/shard_map/all_to_all | solution.py:63
  209.4 8.2 %fusion = bf16[288,3584]{1,0:T(8,128)(2,1)} fusion(f32[288,3584]{1,0:T(8,128)} %fusion.53, bf16[512,3584]{1,0:T(8,128)(2,1)} %collective-permute-done.1, bf16[288,3584]{1,0:T(8,128)(2,1)S(1)} %copy-done.5, bf16[3584,512]{1,0:T(8,128)(2,1)} %collective-permute-done), kind=kOutput, calls=%fused_computation.2 | convolution fusion | flops 2116730880 | bytes 15597568 | tf_op jit(solution)/shard_map/dot_general | solution.py:100
  217.6 4.0 %reshape.200 = bf16[8,36,3584]{2,1,0:T(8,128)(2,1)} reshape(bf16[288,3584]{1,0:T(8,128)(2,1)} %fusion) | data formatting | bytes 4128768 | tf_op jit(solution)/shard_map/reshape | solution.py:101
  221.6 5.3 %all-to-all-start.1 = ((bf16[8,36,3584]{2,1,0:T(8,128)(2,1)}), bf16[8,36,3584]{2,1,0:T(8,128)(2,1)}, u32[]{:S(2)}, u32[]{:S(2)}) async-start(bf16[8,36,3584]{2,1,0:T(8,128)(2,1)} %reshape.200), calls=%async_computation.1 | async-start | bytes 4587520 | tf_op jit(solution)/shard_map/all_to_all | solution.py:63
  226.9 3.5 fusion.54
  230.5 3.5 fusion.1
  236.0 40.7 %all-to-all-done.1 = bf16[8,36,3584]{2,1,0:T(8,128)(2,1)} async-done(((bf16[8,36,3584]{2,1,0:T(8,128)(2,1)}), bf16[8,36,3584]{2,1,0:T(8,128)(2,1)}, u32[]{:S(2)}, u32[]{:S(2)}) %all-to-all-start.1) | async-done | bytes 2064416 | tf_op jit(solution)/shard_map/all_to_all | solution.py:63
  276.7 7.8 %all-to-all-start.5 = ((bf16[8,36,3584]{2,1,0:T(8,128)(2,1)}), bf16[8,36,3584]{2,1,0:T(8,128)(2,1)}, u32[]{:S(2)}, u32[]{:S(2)}) async-start(bf16[8,36,3584]{2,1,0:T(8,128)(2,1)} %reshape.206), calls=%async_computation.5 | async-start | bytes 4587520 | tf_op jit(solution)/shard_map/all_to_all | solution.py:63
  289.3 2.6 reshape.201
  296.9 37.4 %all-to-all-done.5 = bf16[8,36,3584]{2,1,0:T(8,128)(2,1)} async-done(((bf16[8,36,3584]{2,1,0:T(8,128)(2,1)}), bf16[8,36,3584]{2,1,0:T(8,128)(2,1)}, u32[]{:S(2)}, u32[]{:S(2)}) %all-to-all-start.5) | async-done | bytes 2064416 | tf_op jit(solution)/shard_map/all_to_all | solution.py:63
  334.3 2.6 reshape.207
  341.6 22.7 %collective-permute-done.3 = bf16[1,128,3584]{2,1,0:T(8,128)(2,1)S(1)} collective-permute-done((bf16[1,128,3584]{2,1,0:T(8,128)(2,1)S(1)}, bf16[1,128,3584]{2,1,0:T(8,128)(2,1)S(1)}, u32[]{:S(2)}, u32[]{:S(2)}) %collective-permute-start.3) | collective-permute-done | bytes 917536 | tf_op jit(solution)/shard_map/ppermute | solution.py:18
  (96 shorter events, 40.2 us)
Async XLA Ops:
  0.6 284.0 %copy-start = (bf16[1,3584,4]{1,2,0:T(4,128)(2,1)S(1)}, bf16[1,3584,4]{1,2,0:T(4,128)(2,1)}, u32[]{:S(2)}) copy-start(bf16[1,3584,4]{1,2,0:T(4,128)(2,1)} %param.13) | copy-start | bytes 86020
  0.6 3.8 %copy-start.2 = (bf16[1,128,3584]{2,1,0:T(8,128)(2,1)S(1)}, bf16[1,128,3584]{2,1,0:T(8,128)(2,1)}, u32[]{:S(2)}) copy-start(bf16[1,128,3584]{2,1,0:T(8,128)(2,1)} %param.9) | copy-start | bytes 2752516
  7.3 5.5 %copy-start.14 = (s32[1,128,2]{1,2,0:T(2,128)S(1)}, s32[1,128,2]{1,2,0:T(2,128)}, u32[]{:S(2)}) copy-start(s32[1,128,2]{1,2,0:T(2,128)} %param.17) | copy-start | bytes 3076
  7.3 6.3 %copy-start.1 = (bf16[1,128,3584]{2,1,0:T(8,128)(2,1)S(1)}, bf16[1,128,3584]{2,1,0:T(8,128)(2,1)}, u32[]{:S(2)}) copy-start(bf16[1,128,3584]{2,1,0:T(8,128)(2,1)} %param.10) | copy-start | bytes 2752516
  7.3 55.3 %all-to-all-start = ((bf16[8,36,3584]{2,1,0:T(8,128)(2,1)}), bf16[8,36,3584]{2,1,0:T(8,128)(2,1)}, u32[]{:S(2)}, u32[]{:S(2)}) async-start(bf16[8,36,3584]{2,1,0:T(8,128)(2,1)} %reshape.198), calls=%async_computation | async-start | bytes 4587520 | tf_op jit(solution)/shard_map/all_to_all | solution.py:63
  62.6 57.6 %all-to-all-start.2 = ((bf16[8,36,3584]{2,1,0:T(8,128)(2,1)}), bf16[8,36,3584]{2,1,0:T(8,128)(2,1)}, u32[]{:S(2)}, u32[]{:S(2)}) async-start(bf16[8,36,3584]{2,1,0:T(8,128)(2,1)} %reshape.202), calls=%async_computation.2 | async-start | bytes 4587520 | tf_op jit(solution)/shard_map/all_to_all | solution.py:63
  120.2 56.9 %all-to-all-start.3 = ((bf16[8,36,3584]{2,1,0:T(8,128)(2,1)}), bf16[8,36,3584]{2,1,0:T(8,128)(2,1)S(1)}, u32[]{:S(2)}, u32[]{:S(2)}) async-start(bf16[8,36,3584]{2,1,0:T(8,128)(2,1)} %reshape.204), calls=%async_computation.3 | async-start | bytes 4587520 | tf_op jit(solution)/shard_map/all_to_all | solution.py:63
  127.4 66.3 %collective-permute-start = (bf16[3584,512]{1,0:T(8,128)(2,1)}, bf16[3584,512]{1,0:T(8,128)(2,1)}, u32[]{:S(2)}, u32[]{:S(2)}) collective-permute-start(bf16[3584,512]{1,0:T(8,128)(2,1)} %bitcast.111), channel_id=1, source_target_pairs={{0,1},{1,0},{2,3},{3,2},{4,5},{5,4},{6,7},{7,6},{8,9},{9,8},{10,11... | collective-permute-start | bytes 11010056 | tf_op jit(solution)/shard_map/ppermute | solution.py:12
  127.5 70.2 %collective-permute-start.1 = (bf16[512,3584]{1,0:T(8,128)(2,1)}, bf16[512,3584]{1,0:T(8,128)(2,1)}, u32[]{:S(2)}, u32[]{:S(2)}) collective-permute-start(bf16[512,3584]{1,0:T(8,128)(2,1)} %bitcast.118), channel_id=1, source_target_pairs={{0,1},{1,0},{2,3},{3,2},{4,5},{5,4},{6,7},{7,6},{8,9},{9,8},{10,11... | collective-permute-start | bytes 11010056 | tf_op jit(solution)/shard_map/ppermute | solution.py:12
  179.2 4.9 %copy-start.6 = (bf16[288,3584]{1,0:T(8,128)(2,1)S(1)}, bf16[288,3584]{1,0:T(8,128)(2,1)}, u32[]{:S(2)}) copy-start(bf16[288,3584]{1,0:T(8,128)(2,1)} %reshape.205) | copy-start | bytes 6193156
  179.2 4.9 %copy-start.15 = (bf16[1,512,3584]{2,1,0:T(8,128)(2,1)S(1)}, bf16[1,512,3584]{2,1,0:T(8,128)(2,1)}, u32[]{:S(2)}) copy-start(bf16[1,512,3584]{2,1,0:T(8,128)(2,1)} %param.15) | copy-start | bytes 11010052
  184.1 2.1 copy-start.5
  193.7 4.1 %copy-start.7 = (bf16[288,3584]{1,0:T(8,128)(2,1)S(1)}, bf16[288,3584]{1,0:T(8,128)(2,1)}, u32[]{:S(2)}) copy-start(bf16[288,3584]{1,0:T(8,128)(2,1)} %reshape.205) | copy-start | bytes 6193156
  197.7 4.4 %copy-start.8 = (f32[288,512]{1,0:T(8,128)}, f32[288,512]{1,0:T(8,128)S(1)}, u32[]{:S(2)}) copy-start(f32[288,512]{1,0:T(8,128)S(1)} %fusion.105) | copy-start | bytes 1769476
  202.8 18.8 %all-to-all-start.4 = ((f32[8,1,36]{2,1,0:T(1,128)}), f32[8,1,36]{2,1,0:T(1,128)S(1)}, u32[]{:S(2)}, u32[]{:S(2)}) async-start(f32[8,1,36]{2,1,0:T(1,128)} %add.109), calls=%async_computation.4 | async-start | bytes 8192 | tf_op jit(solution)/shard_map/all_to_all | solution.py:63
  221.6 5.3 %copy-start.12 = (f32[288,512]{1,0:T(8,128)S(1)}, f32[288,512]{1,0:T(8,128)}, u32[]{:S(2)}) copy-start(f32[288,512]{1,0:T(8,128)} %copy-done.11) | copy-start | bytes 1769476
  221.6 5.3 %copy-start.13 = (f32[288,512]{1,0:T(8,128)S(1)}, f32[288,512]{1,0:T(8,128)}, u32[]{:S(2)}) copy-start(f32[288,512]{1,0:T(8,128)} %get-tuple-element.23) | copy-start | bytes 1769476
  221.6 55.1 %all-to-all-start.1 = ((bf16[8,36,3584]{2,1,0:T(8,128)(2,1)}), bf16[8,36,3584]{2,1,0:T(8,128)(2,1)}, u32[]{:S(2)}, u32[]{:S(2)}) async-start(bf16[8,36,3584]{2,1,0:T(8,128)(2,1)} %reshape.200), calls=%async_computation.1 | async-start | bytes 4587520 | tf_op jit(solution)/shard_map/all_to_all | solution.py:63
  226.9 3.6 copy-start.9
  226.9 3.6 copy-start.10
  236.0 48.7 %copy-start.3 = (bf16[1,128,3584]{2,1,0:T(8,128)(2,1)S(1)}, bf16[1,128,3584]{2,1,0:T(8,128)(2,1)}, u32[]{:S(2)}) copy-start(bf16[1,128,3584]{2,1,0:T(8,128)(2,1)} %param.9) | copy-start | bytes 2752516
  276.7 57.7 %all-to-all-start.5 = ((bf16[8,36,3584]{2,1,0:T(8,128)(2,1)}), bf16[8,36,3584]{2,1,0:T(8,128)(2,1)}, u32[]{:S(2)}, u32[]{:S(2)}) async-start(bf16[8,36,3584]{2,1,0:T(8,128)(2,1)} %reshape.206), calls=%async_computation.5 | async-start | bytes 4587520 | tf_op jit(solution)/shard_map/all_to_all | solution.py:63
  295.4 46.2 %collective-permute-start.2 = (bf16[1,128,3584]{2,1,0:T(8,128)(2,1)}, bf16[1,128,3584]{2,1,0:T(8,128)(2,1)}, u32[]{:S(2)}, u32[]{:S(2)}) collective-permute-start(bf16[1,128,3584]{2,1,0:T(8,128)(2,1)} %fusion.8), channel_id=1, source_target_pairs={{24,0},{0,8},{8,16},{16,24},{25,1},{1,9},{9,17},{17,25},{26,2},{2,... | collective-permute-start | bytes 2752520 | tf_op jit(solution)/shard_map/ppermute | solution.py:18
  341.0 23.3 %collective-permute-start.3 = (bf16[1,128,3584]{2,1,0:T(8,128)(2,1)S(1)}, bf16[1,128,3584]{2,1,0:T(8,128)(2,1)S(1)}, u32[]{:S(2)}, u32[]{:S(2)}) collective-permute-start(bf16[1,128,3584]{2,1,0:T(8,128)(2,1)S(1)} %fusion.39), channel_id=1, source_target_pairs={{8,0},{16,8},{24,16},{0,24},{9,1},{17,9},{25,17},{1,25},{10,2},{18... | collective-permute-start | bytes 2752520 | tf_op jit(solution)/shard_map/ppermute | solution.py:18
  (2 other events, 2.0 us)

commit v2 on v1

--- a/solution.py
+++ b/solution.py
@@ -35,18 +35,124 @@
     return (onehot, picked, total, ROUTE_SCALE * picked / total)
 
 
-def slot_masks(choose, experts, capacity):
+ROWS = 16
+
+
+class Layout:
+    def __init__(self, width, half_cap, devices):
+        self.width, self.half_cap, self.devices = width, half_cap, devices
+        self.full, self.left = half_cap // ROWS, half_cap % ROWS
+        self.pieces = ROWS // self.left if self.left else 1
+        if self.left and (ROWS % self.left or width % (128 * self.pieces)):
+            self.full, self.left, self.pieces = self.full + 1, 0, 1
+        self.part = width // self.pieces
+        self.columns = self.full * width + (self.part if self.left else 0)
+
+    def masks(self, where):
+        block = jnp.arange(self.devices * ROWS, dtype=jnp.int32)
+        to, row = lax.axis_index("expert") ^ (block // ROWS), block % ROWS
+        first = to * self.half_cap
+        found = []
+        for group in range(self.full):
+            slot = group * ROWS + row
+            place = jnp.where(slot < self.half_cap, first + slot, -1)
+            found.append((place[:, None] == where[None, :]).astype(jnp.bfloat16))
+        for piece in range(self.pieces if self.left else 0):
+            slot = self.full * ROWS + row % self.left
+            place = jnp.where(row // self.left == piece, first + slot, -1)
+            found.append((place[:, None] == where[None, :]).astype(jnp.bfloat16))
+        return found
+
+    def parts(self, rows):
+        return [rows[:, c * self.part : (c + 1) * self.part] for c in range(self.pieces)]
+
+    def dispatch(self, masks, rows):
+        cols = [pick(m, rows) for m in masks[: self.full]]
+        if self.left:
+            cols.append(
+                pick(
+                    jnp.concatenate(masks[self.full :], axis=1),
+                    jnp.concatenate(self.parts(rows), axis=0),
+                )
+            )
+        return jnp.concatenate(cols, axis=1)
+
+    def lifts(self):
+        slot = jnp.arange(self.devices * self.left, dtype=jnp.int32)
+        block = jnp.arange(self.devices * ROWS, dtype=jnp.int32)
+        at = (slot // self.left) * ROWS + slot % self.left
+        return [
+            (at[:, None] + c * self.left == block[None, :]).astype(jnp.bfloat16)
+            for c in range(self.pieces)
+        ]
+
+    def unpack(self, packed):
+        rows = [packed[:, g * self.width : (g + 1) * self.width] for g in range(self.full)]
+        if self.left:
+            tail = packed[:, self.full * self.width : self.columns]
+            rows.append(jnp.concatenate([pick(m, tail) for m in self.lifts()], axis=1))
+        return jnp.concatenate(rows, axis=0)
+
+    def pack(self, rows):
+        size = self.devices * ROWS
+        cols = [rows[g * size : (g + 1) * size] for g in range(self.full)]
+        if self.left:
+            tail = rows[self.full * size :]
+            cols.append(
+                sum(back_to_tokens(m, p) for m, p in zip(self.lifts(), self.parts(tail))).astype(
+                    jnp.bfloat16
+                )
+            )
+        return jnp.concatenate(cols, axis=1)
+
+    def numbers(self, values):
+        size = self.devices * ROWS
+        cols = [values[g * size : (g + 1) * size] for g in range(self.full)]
+        if self.left:
+            tail = values[self.full * size :]
+            cols.append(jnp.sum(self.lifts()[0].astype(jnp.float32) * tail[:, None], axis=0))
+        both = jnp.stack(cols, axis=1)
+        high = lax.reduce_precision(both, 8, 7)
+        split = jnp.concatenate([high, both - high], axis=1)
+        return jnp.pad(split, ((0, 0), (0, -split.shape[1] % 128))).astype(jnp.bfloat16)
+
+    def numbers_home(self, masks, split):
+        count = self.full + (1 if self.left else 0)
+        wide = split.astype(jnp.float32)
+        return sum(
+            jnp.sum(masks[g].astype(jnp.float32) * (wide[:, g] + wide[:, count + g])[:, None], axis=0)
+            for g in range(count)
+        )
+
+    def home(self, masks, packed):
+        out = sum(
+            back_to_tokens(masks[g], packed[:, g * self.width : (g + 1) * self.width])
+            for g in range(self.full)
+        )
+        if self.left:
+            tail = packed[:, self.full * self.width : self.columns]
+            out = out + jnp.concatenate(
+                [back_to_tokens(m, tail) for m in masks[self.full :]], axis=1
+            )
+        return out
+
+    def swap(self, packed):
+        got = [packed[:ROWS]]
+        for j in range(1, self.devices):
+            route = [(i, i ^ j) for i in range(self.devices)]
+            got.append(lax.ppermute(packed[j * ROWS : (j + 1) * ROWS], "expert", route))
+        return jnp.concatenate(got, axis=0)
+
+
+def slots_of(choose, experts, capacity):
     tok_rows, top = choose.shape
     flat = choose.reshape(-1)
-    count = tok_rows * top
     onehot = (flat[:, None] == jnp.arange(experts, dtype=jnp.int32)[None, :]).astype(jnp.bfloat16)
-    at = jnp.arange(count, dtype=jnp.int32)
+    at = jnp.arange(tok_rows * top, dtype=jnp.int32)
     earlier = (at[None, :] < at[:, None]).astype(jnp.bfloat16)
     before = jnp.dot(earlier, onehot, preferred_element_type=jnp.float32)
     slot = jnp.sum(before * onehot.astype(jnp.float32), axis=1).astype(jnp.int32)
-    where = (flat * capacity + slot).reshape(tok_rows, top)
-    places = jnp.arange(experts * capacity, dtype=jnp.int32)
-    return [(places[:, None] == where[None, :, k]).astype(jnp.bfloat16) for k in range(top)]
+    return (flat * capacity + slot).reshape(tok_rows, top)
 
 
 def pick(mask, rows):
@@ -54,13 +160,7 @@
 
 
 def back_to_tokens(mask, rows):
-    return lax.dot_general(
-        mask, rows, (((0,), (0,)), ((), ())), preferred_element_type=jnp.float32
-    )
-
-
-def swap(rows):
-    return lax.all_to_all(rows, "expert", split_axis=0, concat_axis=0, tiled=True)
+    return lax.dot_general(mask, rows, (((0,), (0,)), ((), ())), preferred_element_type=jnp.float32)
 
 
 def on_device(
@@ -75,33 +175,36 @@
     capacity = 9 * tok_rows * top // (8 * experts)
     half_cap = capacity // HALVES
     devices = lax.axis_size("expert")
-    shape = (devices, half_cap, width)
+    plan = Layout(width, half_cap, devices)
     ups = [w_up[0], partner(w_up[0], "expert", 0)]
     downs = [w_down[0], partner(w_down[0], "expert", 0)]
 
     choose_a = fwd_experts[0]
-    masks_a = slot_masks(choose_a, experts, capacity)
+    where_a = slots_of(choose_a, experts, capacity)
+    masks_a = [plan.masks(where_a[:, k]) for k in range(top)]
     wide_a, inv_a, normed_a = normalize(fwd_acts[0], gain)
-    got_a = swap(pick(sum(masks_a), normed_a).reshape(shape)).reshape(-1, width)
+    spread_a = [sum(each) for each in zip(*masks_a)]
+    got_a = plan.unpack(plan.swap(plan.dispatch(spread_a, normed_a)))
     _, _, _, gate_a = gating(normed_a, table, choose_a)
 
     choose_b = bwd_experts[0]
     grads_b = bwd_grads[0]
-    masks_b = slot_masks(choose_b, experts, capacity)
+    where_b = slots_of(choose_b, experts, capacity)
+    masks_b = [plan.masks(where_b[:, k]) for k in range(top)]
     wide_b, inv_b, normed_b = normalize(bwd_saved[0], gain)
-    spread = sum(masks_b)
-    got_x = swap(pick(spread, normed_b).reshape(shape)).reshape(-1, width)
-    got_g = swap(pick(spread, grads_b).reshape(shape)).reshape(-1, width)
+    spread_b = [sum(each) for each in zip(*masks_b)]
+    got_x = plan.unpack(plan.swap(plan.dispatch(spread_b, normed_b)))
+    got_g = plan.unpack(plan.swap(plan.dispatch(spread_b, grads_b)))
     onehot_b, picked_b, total_b, gate_b = gating(normed_b, table, choose_b)
 
-    y = jnp.zeros((devices * half_cap, width), jnp.float32)
+    y = jnp.zeros((got_a.shape[0], width), jnp.float32)
     for up, down in zip(ups, downs):
         hidden = jax.nn.silu(jnp.dot(got_a, up, preferred_element_type=jnp.float32))
         y += jnp.dot(hidden.astype(jnp.bfloat16), down, preferred_element_type=jnp.float32)
-    back_a = swap(y.astype(jnp.bfloat16).reshape(shape)).reshape(-1, width)
-
-    dx = jnp.zeros((devices * half_cap, width), jnp.float32)
-    dgate_rows = jnp.zeros((devices * half_cap,), jnp.float32)
+    back_a = plan.swap(plan.pack(y.astype(jnp.bfloat16)))
+
+    dx = jnp.zeros((got_a.shape[0], width), jnp.float32)
+    dgate_rows = jnp.zeros((got_a.shape[0],), jnp.float32)
     for up, down in zip(ups, downs):
         pre = jnp.dot(got_x, up, preferred_element_type=jnp.float32)
         sigma = jax.nn.sigmoid(pre)
@@ -112,24 +215,24 @@
         dgate_rows += jnp.sum(hidden * back, axis=1)
         dpre = (back * sigma * (1.0 + pre * (1.0 - sigma))).astype(jnp.bfloat16)
         dx += lax.dot_general(dpre, up, (((1,), (1,)), ((), ())), preferred_element_type=jnp.float32)
-    back_g = swap(dgate_rows.reshape(devices, half_cap)).reshape(-1)
-    back_x = swap(dx.astype(jnp.bfloat16).reshape(shape)).reshape(-1, width)
+    back_x = plan.swap(
+        jnp.concatenate([plan.pack(dx.astype(jnp.bfloat16)), plan.numbers(dgate_rows)], axis=1)
+    )
 
     out_a = wide_a
     for k in range(top):
-        out_a = out_a + gate_a[:, k : k + 1] * back_to_tokens(masks_a[k], back_a)
+        out_a = out_a + gate_a[:, k : k + 1] * plan.home(masks_a[k], back_a)
     fwd_next = passed_along(out_a.astype(jnp.bfloat16)[None], "pipe", 1)
 
-    dgate = jnp.stack(
-        [jnp.sum(m.astype(jnp.float32) * back_g[:, None], axis=0) for m in masks_b], axis=1
-    )
+    split = back_x[:, plan.columns :]
+    dgate = jnp.stack([plan.numbers_home(m, split) for m in masks_b], axis=1)
     dsel = ROUTE_SCALE / total_b * (
         dgate - jnp.sum(dgate * picked_b, axis=1, keepdims=True) / total_b
     )
     dlogit = jnp.sum(onehot_b * (dsel * picked_b * (1.0 - picked_b))[:, :, None], axis=1)
     dnormed = jnp.dot(dlogit, table.astype(jnp.float32).T, precision=lax.Precision.HIGHEST)
     for k in range(top):
-        dnormed = dnormed + gate_b[:, k : k + 1] * back_to_tokens(masks_b[k], back_x)
+        dnormed = dnormed + gate_b[:, k : k + 1] * plan.home(masks_b[k], back_x)
     scaled = dnormed * gain
     inner = jnp.mean(scaled * wide_b, axis=-1, keepdims=True)
     dx_b = grads_b.astype(jnp.float32) + inv_b * scaled - wide_b * inv_b**3 * inner

time: 372 us -> 366 us (0.984)
  matrix products: 50.8 us -> 73.5 us
  waiting for transfers between devices: 234 us -> 217 us
  starting transfers between devices: 42.8 us -> 30 us
  other arithmetic: 4.27 us -> 8.35 us
    all_to_all x6 -> x0, waiting for transfers between devices: 211 us -> none  [swap(): lax.all_to_all(rows, 'expert', split_axis=0, concat_axis=0, tiled=True)]
    ppermute x0 -> x35, waiting for transfers between devices: none -> 194 us  [swap(): got.append(lax.ppermute(packed[j * ROWS:(j + 1) * ROWS], 'expert', route))]
    all_to_all x6 -> x0, starting transfers between devices: 40.2 us -> none  [swap(): lax.all_to_all(rows, 'expert', split_axis=0, concat_axis=0, tiled=True)]
    ppermute x0 -> x35, starting transfers between devices: none -> 27.6 us  [swap(): got.append(lax.ppermute(packed[j * ROWS:(j + 1) * ROWS], 'expert', route))]
    reshape x10 -> x0, local copies, waits for them, and re-layouts: 27.5 us -> none  [the longest x2 6.53 us: on_device(): back_a = swap(y.astype(jnp.bfloat16).reshape(shape)).reshape(-1, width)]
    slice x2 -> x14, local copies, waits for them, and re-layouts: 0.35 us -> 14.5 us  [the longest x2 4.22 us: pack(): cols = [rows[g * size:(g + 1) * size] for g in range(self.full)]]
    dot_general x4 -> x32, matrix products: 6.66 us -> 18 us  [back_to_tokens(): lax.dot_general(mask, rows, (((0,), (0,)), ((), ())), preferred_element_t...]
    unnamed x36 -> x206, local copies, waits for them, and re-layouts: 5.05 us -> 15.5 us
  transfers between devices with their start and end apart: 10 -> 39, of which waited for: 6 -> 22; matrix products, arithmetic and copies ran while one was open for 20% -> 20% of each run, Pallas kernels for 0% -> 0%
where the time goes in v2:
time: 366 us; the launch traced here: 365 us
  waiting for transfers between devices  217 us (59%)
  matrix products  73.5 us (20%)
  local copies, waits for them, and re-layouts  33.4 us (9%)
  starting transfers between devices  30 us (8%)
  other arithmetic  8.35 us (2%)
    ppermute x35, waiting for transfers between devices, swap(): got.append(lax.ppermute(packed[j * ROWS:(j + 1) * ROWS], 'expert', route))  194 us
    ppermute x35, starting transfers between devices, swap(): got.append(lax.ppermute(packed[j * ROWS:(j + 1) * ROWS], 'expert', route))  27.6 us
    ppermute x2, waiting for transfers between devices, passed_along(): return lax.ppermute(block, axis, route)  23 us
    dot_general x32, matrix products, back_to_tokens(): lax.dot_general(mask, rows, (((0,), (0,)), ((), ())), preferred_element_t...  18 us
    dot_general x2, matrix products, on_device(): jnp.dot(hidden.astype(jnp.bfloat16), down, preferred_element_type=jnp.flo...  17 us
    unnamed x206, local copies, waits for them, and re-layouts  15.5 us
    dot_general x21, matrix products, pick(): jnp.dot(mask, rows, preferred_element_type=jnp.float32).astype(jnp.bfloat16)  11.8 us
    dot_general x2, matrix products, on_device(): lax.dot_general(dpre, up, (((1,), (1,)), ((), ())), preferred_element_typ...  9.1 us
  transfers between devices with their start and end apart: 39, of which 22 were waited for; matrix products, arithmetic and copies ran while one was open for 20% of the time, Pallas kernels for 0%

profile of v2, /device:TPU:10, one launch (start us, length us, event | category | flops | bytes accessed | tf_op | source)
XLA Modules:
  0.0 365.0 jit_solution(6968267814782176020)
XLA Ops:
  39.8 8.0 %collective-permute-done.21 = bf16[16,8064]{1,0:T(8,128)(2,1)} collective-permute-done((bf16[16,8064]{1,0:T(8,128)(2,1)}, bf16[16,8064]{1,0:T(8,128)(2,1)}, u32[]{:S(2)}, u32[]{:S(2)}) %collective-permute-start.21) | collective-permute-done | bytes 258080 | tf_op jit(solution)/shard_map/ppermute | solution.py:143
  54.0 10.3 %collective-permute-done.23 = bf16[16,8064]{1,0:T(8,128)(2,1)S(1)} collective-permute-done((bf16[16,8064]{1,0:T(8,128)(2,1)}, bf16[16,8064]{1,0:T(8,128)(2,1)S(1)}, u32[]{:S(2)}, u32[]{:S(2)}) %collective-permute-start.23) | collective-permute-done | bytes 258080 | tf_op jit(solution)/shard_map/ppermute | solution.py:143
  69.2 17.1 %collective-permute-done.27 = bf16[16,8064]{1,0:T(8,128)(2,1)S(1)} collective-permute-done((bf16[16,8064]{1,0:T(8,128)(2,1)S(1)}, bf16[16,8064]{1,0:T(8,128)(2,1)S(1)}, u32[]{:S(2)}, u32[]{:S(2)}) %collective-permute-start.27) | collective-permute-done | bytes 258080 | tf_op jit(solution)/shard_map/ppermute | solution.py:143
  86.4 5.5 %collective-permute-done.28 = bf16[16,8064]{1,0:T(8,128)(2,1)S(1)} collective-permute-done((bf16[16,8064]{1,0:T(8,128)(2,1)S(1)}, bf16[16,8064]{1,0:T(8,128)(2,1)S(1)}, u32[]{:S(2)}, u32[]{:S(2)}) %collective-permute-start.28) | collective-permute-done | bytes 258080 | tf_op jit(solution)/shard_map/ppermute | solution.py:143
  91.9 5.5 %collective-permute-done.29 = bf16[16,8064]{1,0:T(8,128)(2,1)S(1)} collective-permute-done((bf16[16,8064]{1,0:T(8,128)(2,1)S(1)}, bf16[16,8064]{1,0:T(8,128)(2,1)S(1)}, u32[]{:S(2)}, u32[]{:S(2)}) %collective-permute-start.29) | collective-permute-done | bytes 258080 | tf_op jit(solution)/shard_map/ppermute | solution.py:143
  97.4 4.9 %collective-permute-done.30 = bf16[16,8064]{1,0:T(8,128)(2,1)S(1)} collective-permute-done((bf16[16,8064]{1,0:T(8,128)(2,1)S(1)}, bf16[16,8064]{1,0:T(8,128)(2,1)S(1)}, u32[]{:S(2)}, u32[]{:S(2)}) %collective-permute-start.30) | collective-permute-done | bytes 258080 | tf_op jit(solution)/shard_map/ppermute | solution.py:143
  106.4 7.1 %collective-permute-done.2 = bf16[16,8064]{1,0:T(8,128)(2,1)S(1)} collective-permute-done((bf16[16,8064]{1,0:T(8,128)(2,1)S(1)}, bf16[16,8064]{1,0:T(8,128)(2,1)S(1)}, u32[]{:S(2)}, u32[]{:S(2)}) %collective-permute-start.2) | collective-permute-done | bytes 258080 | tf_op jit(solution)/shard_map/ppermute | solution.py:143
  115.8 13.7 %collective-permute-done.3 = bf16[16,8064]{1,0:T(8,128)(2,1)S(1)} collective-permute-done((bf16[16,8064]{1,0:T(8,128)(2,1)S(1)}, bf16[16,8064]{1,0:T(8,128)(2,1)S(1)}, u32[]{:S(2)}, u32[]{:S(2)}) %collective-permute-start.3) | collective-permute-done | bytes 258080 | tf_op jit(solution)/shard_map/ppermute | solution.py:143
  130.9 9.6 %collective-permute-done.4 = bf16[16,8064]{1,0:T(8,128)(2,1)S(1)} collective-permute-done((bf16[16,8064]{1,0:T(8,128)(2,1)S(1)}, bf16[16,8064]{1,0:T(8,128)(2,1)S(1)}, u32[]{:S(2)}, u32[]{:S(2)}) %collective-permute-start.4) | collective-permute-done | bytes 258080 | tf_op jit(solution)/shard_map/ppermute | solution.py:143
  142.0 4.1 %collective-permute-done.5 = bf16[16,8064]{1,0:T(8,128)(2,1)S(1)} collective-permute-done((bf16[16,8064]{1,0:T(8,128)(2,1)S(1)}, bf16[16,8064]{1,0:T(8,128)(2,1)S(1)}, u32[]{:S(2)}, u32[]{:S(2)}) %collective-permute-start.5) | collective-permute-done | bytes 258080 | tf_op jit(solution)/shard_map/ppermute | solution.py:143
  155.1 4.0 %multiply_reduce_fusion.1 = (f32[288]{0:T(512)}, f32[288,512]{1,0:T(8,128)S(1)}) fusion(f32[288,512]{1,0:T(8,128)S(1)} %fusion.314, bf16[1,512,3584]{2,1,0:T(8,128)(2,1)} %param.15, bf16[32,896]{1,0:T(8,128)(2,1)S(1)} %convolution_convert_fusion.13, bf16[32,896]{1,0:T(8,128)(2,1)S(1)} %convolution_convert_fusion.14, ...), kind=kOutput, calls=%fused_computation.140 | convolution fusion | flops 1070530304 | bytes 6915200 | tf_op jit(solution)/shard_map/dot_general | solution.py:212
  159.1 5.6 %fusion.92 = f32[288,3584]{1,0:T(8,128)} fusion(f32[288,512]{1,0:T(8,128)S(1)} %fusion.314, f32[288,512]{1,0:T(8,128)S(1)} %get-tuple-element.116, bf16[1,3584,512]{2,1,0:T(8,128)(2,1)} %param.14), kind=kOutput, calls=%fused_computation.149 | convolution fusion | flops 1058291712 | bytes 8978432 | tf_op jit(solution)/shard_map/dot_general | solution.py:217
  166.1 8.2 %fusion.91 = f32[288,3584]{1,0:T(8,128)} fusion(bf16[1,512,3584]{2,1,0:T(8,128)(2,1)} %param.15, bf16[1,3584,512]{2,1,0:T(8,128)(2,1)} %param.14, bf16[32,896]{1,0:T(8,128)(2,1)S(1)} %convolution_convert_fusion.17, bf16[32,896]{1,0:T(8,128)(2,1)S(1)} %convolution_convert_fusion.18, bf16[32,896]{1,0:T(8,128)(2,1)S(1)} %convolution_convert_fusion.19, ...), kind=kOutput, calls=%fused_computation.148 | convolution fusion | flops 2127052800 | bytes 13533184 | tf_op jit(solution)/shard_map/dot_general | solution.py:203
  187.9 8.8 %fusion = bf16[288,3584]{1,0:T(8,128)(2,1)} fusion(f32[288,3584]{1,0:T(8,128)} %fusion.91, bf16[512,3584]{1,0:T(8,128)(2,1)} %collective-permute-done.8, bf16[3584,512]{1,0:T(8,128)(2,1)} %collective-permute-done.7, bf16[32,896]{1,0:T(8,128)(2,1)S(1)} %convolution_convert_fusion.17, bf16[32,896]{1,0:T(8,128)(2,1)} %copy-done.34, ...), kind=kOutput, calls=%fused_computation.2 | convolution fusion | flops 2129117184 | bytes 15597568 | tf_op jit(solution)/shard_map/dot_general | solution.py:203
  215.3 20.7 %collective-permute-done.10 = bf16[16,8064]{1,0:T(8,128)(2,1)S(1)} collective-permute-done((bf16[16,8064]{1,0:T(8,128)(2,1)S(1)}, bf16[16,8064]{1,0:T(8,128)(2,1)S(1)}, u32[]{:S(2)}, u32[]{:S(2)}) %collective-permute-start.10) | collective-permute-done | bytes 258080 | tf_op jit(solution)/shard_map/ppermute | solution.py:143
  236.1 8.3 %collective-permute-done.11 = bf16[16,8064]{1,0:T(8,128)(2,1)S(1)} collective-permute-done((bf16[16,8064]{1,0:T(8,128)(2,1)S(1)}, bf16[16,8064]{1,0:T(8,128)(2,1)S(1)}, u32[]{:S(2)}, u32[]{:S(2)}) %collective-permute-start.11) | collective-permute-done | bytes 258080 | tf_op jit(solution)/shard_map/ppermute | solution.py:143
  245.4 11.3 %collective-permute-done.12 = bf16[16,8064]{1,0:T(8,128)(2,1)S(1)} collective-permute-done((bf16[16,8064]{1,0:T(8,128)(2,1)S(1)}, bf16[16,8064]{1,0:T(8,128)(2,1)S(1)}, u32[]{:S(2)}, u32[]{:S(2)}) %collective-permute-start.12) | collective-permute-done | bytes 258080 | tf_op jit(solution)/shard_map/ppermute | solution.py:143
  259.4 10.3 %collective-permute-done.13 = bf16[16,8064]{1,0:T(8,128)(2,1)S(1)} collective-permute-done((bf16[16,8064]{1,0:T(8,128)(2,1)S(1)}, bf16[16,8064]{1,0:T(8,128)(2,1)S(1)}, u32[]{:S(2)}, u32[]{:S(2)}) %collective-permute-start.13) | collective-permute-done | bytes 258080 | tf_op jit(solution)/shard_map/ppermute | solution.py:143
  271.2 12.3 %collective-permute-done.14 = bf16[16,8064]{1,0:T(8,128)(2,1)S(1)} collective-permute-done((bf16[16,8064]{1,0:T(8,128)(2,1)S(1)}, bf16[16,8064]{1,0:T(8,128)(2,1)S(1)}, u32[]{:S(2)}, u32[]{:S(2)}) %collective-permute-start.14) | collective-permute-done | bytes 258080 | tf_op jit(solution)/shard_map/ppermute | solution.py:143
  284.1 12.9 %collective-permute-done.15 = bf16[16,8064]{1,0:T(8,128)(2,1)S(1)} collective-permute-done((bf16[16,8064]{1,0:T(8,128)(2,1)S(1)}, bf16[16,8064]{1,0:T(8,128)(2,1)S(1)}, u32[]{:S(2)}, u32[]{:S(2)}) %collective-permute-start.15) | collective-permute-done | bytes 258080 | tf_op jit(solution)/shard_map/ppermute | solution.py:143
  305.7 14.7 %collective-permute-done.35 = bf16[16,8192]{1,0:T(8,128)(2,1)S(1)} collective-permute-done((bf16[16,8192]{1,0:T(8,128)(2,1)S(1)}, bf16[16,8192]{1,0:T(8,128)(2,1)S(1)}, u32[]{:S(2)}, u32[]{:S(2)}) %collective-permute-start.35) | collective-permute-done | bytes 262176 | tf_op jit(solution)/shard_map/ppermute | solution.py:143
  320.5 6.7 %collective-permute-done.36 = bf16[16,8192]{1,0:T(8,128)(2,1)S(1)} collective-permute-done((bf16[16,8192]{1,0:T(8,128)(2,1)S(1)}, bf16[16,8192]{1,0:T(8,128)(2,1)S(1)}, u32[]{:S(2)}, u32[]{:S(2)}) %collective-permute-start.36) | collective-permute-done | bytes 262176 | tf_op jit(solution)/shard_map/ppermute | solution.py:143
  327.2 4.5 %collective-permute-done.37 = bf16[16,8192]{1,0:T(8,128)(2,1)S(1)} collective-permute-done((bf16[16,8192]{1,0:T(8,128)(2,1)S(1)}, bf16[16,8192]{1,0:T(8,128)(2,1)S(1)}, u32[]{:S(2)}, u32[]{:S(2)}) %collective-permute-start.37) | collective-permute-done | bytes 262176 | tf_op jit(solution)/shard_map/ppermute | solution.py:143
  340.1 23.0 %collective-permute-done.38 = bf16[1,128,3584]{2,1,0:T(8,128)(2,1)S(1)} collective-permute-done((bf16[1,128,3584]{2,1,0:T(8,128)(2,1)S(1)}, bf16[1,128,3584]{2,1,0:T(8,128)(2,1)S(1)}, u32[]{:S(2)}, u32[]{:S(2)}) %collective-permute-start.38) | collective-permute-done | bytes 917536 | tf_op jit(solution)/shard_map/ppermute | solution.py:18
  (396 shorter events, 125.5 us)
Async XLA Ops:
  9.1 24.8 %collective-permute-start.19 = (bf16[16,8064]{1,0:T(8,128)(2,1)}, bf16[16,8064]{1,0:T(8,128)(2,1)}, u32[]{:S(2)}, u32[]{:S(2)}) collective-permute-start(bf16[16,8064]{1,0:T(8,128)(2,1)} %get-tuple-element.51), channel_id=1, source_target_pairs={{0,3},{1,2},{2,1},{3,0},{4,7},{5,6},{6,5},{7,4},{8,11},{9,10},{10,... | collective-permute-start | bytes 774152 | tf_op jit(solution)/shard_map/ppermute | solution.py:143
  10.5 25.3 %collective-permute-start.20 = (bf16[16,8064]{1,0:T(8,128)(2,1)}, bf16[16,8064]{1,0:T(8,128)(2,1)}, u32[]{:S(2)}, u32[]{:S(2)}) collective-permute-start(bf16[16,8064]{1,0:T(8,128)(2,1)} %get-tuple-element.50), channel_id=1, source_target_pairs={{0,4},{1,5},{2,6},{3,7},{4,0},{5,1},{6,2},{7,3},{8,12},{9,13},{10,... | collective-permute-start | bytes 774152 | tf_op jit(solution)/shard_map/ppermute | solution.py:143
  13.1 34.6 %collective-permute-start.21 = (bf16[16,8064]{1,0:T(8,128)(2,1)}, bf16[16,8064]{1,0:T(8,128)(2,1)}, u32[]{:S(2)}, u32[]{:S(2)}) collective-permute-start(bf16[16,8064]{1,0:T(8,128)(2,1)} %get-tuple-element.49), channel_id=1, source_target_pairs={{0,5},{1,4},{2,7},{3,6},{4,1},{5,0},{6,3},{7,2},{8,13},{9,12},{10,... | collective-permute-start | bytes 774152 | tf_op jit(solution)/shard_map/ppermute | solution.py:143
  28.7 24.5 %collective-permute-start.22 = (bf16[16,8064]{1,0:T(8,128)(2,1)}, bf16[16,8064]{1,0:T(8,128)(2,1)S(1)}, u32[]{:S(2)}, u32[]{:S(2)}) collective-permute-start(bf16[16,8064]{1,0:T(8,128)(2,1)} %get-tuple-element.48), channel_id=1, source_target_pairs={{0,6},{1,7},{2,4},{3,5},{4,2},{5,3},{6,0},{7,1},{8,14},{9,15},{10,... | collective-permute-start | bytes 774152 | tf_op jit(solution)/shard_map/ppermute | solution.py:143
  31.9 32.4 %collective-permute-start.23 = (bf16[16,8064]{1,0:T(8,128)(2,1)}, bf16[16,8064]{1,0:T(8,128)(2,1)S(1)}, u32[]{:S(2)}, u32[]{:S(2)}) collective-permute-start(bf16[16,8064]{1,0:T(8,128)(2,1)} %get-tuple-element.47), channel_id=1, source_target_pairs={{0,7},{1,6},{2,5},{3,4},{4,3},{5,2},{6,1},{7,0},{8,15},{9,14},{10,... | collective-permute-start | bytes 774152 | tf_op jit(solution)/shard_map/ppermute | solution.py:143
  33.9 32.9 %collective-permute-start.24 = (bf16[16,8064]{1,0:T(8,128)(2,1)}, bf16[16,8064]{1,0:T(8,128)(2,1)S(1)}, u32[]{:S(2)}, u32[]{:S(2)}) collective-permute-start(bf16[16,8064]{1,0:T(8,128)(2,1)} %get-tuple-element.43), channel_id=1, source_target_pairs={{0,1},{1,0},{2,3},{3,2},{4,5},{5,4},{6,7},{7,6},{8,9},{9,8},{10,11... | collective-permute-start | bytes 774152 | tf_op jit(solution)/shard_map/ppermute | solution.py:143
  35.8 32.1 %collective-permute-start.25 = (bf16[16,8064]{1,0:T(8,128)(2,1)}, bf16[16,8064]{1,0:T(8,128)(2,1)S(1)}, u32[]{:S(2)}, u32[]{:S(2)}) collective-permute-start(bf16[16,8064]{1,0:T(8,128)(2,1)} %get-tuple-element.42), channel_id=1, source_target_pairs={{0,2},{1,3},{2,0},{3,1},{4,6},{5,7},{6,4},{7,5},{8,10},{9,11},{10,... | collective-permute-start | bytes 774152 | tf_op jit(solution)/shard_map/ppermute | solution.py:143
  53.3 33.1 %collective-permute-start.27 = (bf16[16,8064]{1,0:T(8,128)(2,1)S(1)}, bf16[16,8064]{1,0:T(8,128)(2,1)S(1)}, u32[]{:S(2)}, u32[]{:S(2)}) collective-permute-start(bf16[16,8064]{1,0:T(8,128)(2,1)S(1)} %copy-done.30), channel_id=1, source_target_pairs={{0,4},{1,5},{2,6},{3,7},{4,0},{5,1},{6,2},{7,3},{8,12},{9,13},{10,... | collective-permute-start | bytes 774152 | tf_op jit(solution)/shard_map/ppermute | solution.py:143
  64.3 27.5 %collective-permute-start.28 = (bf16[16,8064]{1,0:T(8,128)(2,1)S(1)}, bf16[16,8064]{1,0:T(8,128)(2,1)S(1)}, u32[]{:S(2)}, u32[]{:S(2)}) collective-permute-start(bf16[16,8064]{1,0:T(8,128)(2,1)S(1)} %copy-done.29), channel_id=1, source_target_pairs={{0,5},{1,4},{2,7},{3,6},{4,1},{5,0},{6,3},{7,2},{8,13},{9,12},{10,... | collective-permute-start | bytes 774152 | tf_op jit(solution)/shard_map/ppermute | solution.py:143
  66.8 30.6 %collective-permute-start.29 = (bf16[16,8064]{1,0:T(8,128)(2,1)S(1)}, bf16[16,8064]{1,0:T(8,128)(2,1)S(1)}, u32[]{:S(2)}, u32[]{:S(2)}) collective-permute-start(bf16[16,8064]{1,0:T(8,128)(2,1)S(1)} %copy-done.28), channel_id=1, source_target_pairs={{0,6},{1,7},{2,4},{3,5},{4,2},{5,3},{6,0},{7,1},{8,14},{9,15},{10,... | collective-permute-start | bytes 774152 | tf_op jit(solution)/shard_map/ppermute | solution.py:143
  68.0 34.3 %collective-permute-start.30 = (bf16[16,8064]{1,0:T(8,128)(2,1)S(1)}, bf16[16,8064]{1,0:T(8,128)(2,1)S(1)}, u32[]{:S(2)}, u32[]{:S(2)}) collective-permute-start(bf16[16,8064]{1,0:T(8,128)(2,1)S(1)} %copy-done.26), channel_id=1, source_target_pairs={{0,7},{1,6},{2,5},{3,4},{4,3},{5,2},{6,1},{7,0},{8,15},{9,14},{10,... | collective-permute-start | bytes 774152 | tf_op jit(solution)/shard_map/ppermute | solution.py:143
  68.8 105.5 %collective-permute-start.7 = (bf16[3584,512]{1,0:T(8,128)(2,1)}, bf16[3584,512]{1,0:T(8,128)(2,1)}, u32[]{:S(2)}, u32[]{:S(2)}) collective-permute-start(bf16[3584,512]{1,0:T(8,128)(2,1)} %bitcast.5), channel_id=1, source_target_pairs={{0,1},{1,0},{2,3},{3,2},{4,5},{5,4},{6,7},{7,6},{8,9},{9,8},{10,11... | collective-permute-start | bytes 11010056 | tf_op jit(solution)/shard_map/ppermute | solution.py:12
  86.3 91.5 %collective-permute-start.8 = (bf16[512,3584]{1,0:T(8,128)(2,1)}, bf16[512,3584]{1,0:T(8,128)(2,1)}, u32[]{:S(2)}, u32[]{:S(2)}) collective-permute-start(bf16[512,3584]{1,0:T(8,128)(2,1)} %bitcast.6), channel_id=1, source_target_pairs={{0,1},{1,0},{2,3},{3,2},{4,5},{5,4},{6,7},{7,6},{8,9},{9,8},{10,11... | collective-permute-start | bytes 11010056 | tf_op jit(solution)/shard_map/ppermute | solution.py:12
  103.2 26.3 %collective-permute-start.3 = (bf16[16,8064]{1,0:T(8,128)(2,1)S(1)}, bf16[16,8064]{1,0:T(8,128)(2,1)S(1)}, u32[]{:S(2)}, u32[]{:S(2)}) collective-permute-start(bf16[16,8064]{1,0:T(8,128)(2,1)S(1)} %copy-done.23), channel_id=1, source_target_pairs={{0,4},{1,5},{2,6},{3,7},{4,0},{5,1},{6,2},{7,3},{8,12},{9,13},{10,... | collective-permute-start | bytes 774152 | tf_op jit(solution)/shard_map/ppermute | solution.py:143
  106.3 34.2 %collective-permute-start.4 = (bf16[16,8064]{1,0:T(8,128)(2,1)S(1)}, bf16[16,8064]{1,0:T(8,128)(2,1)S(1)}, u32[]{:S(2)}, u32[]{:S(2)}) collective-permute-start(bf16[16,8064]{1,0:T(8,128)(2,1)S(1)} %copy-done.22), channel_id=1, source_target_pairs={{0,5},{1,4},{2,7},{3,6},{4,1},{5,0},{6,3},{7,2},{8,13},{9,12},{10,... | collective-permute-start | bytes 774152 | tf_op jit(solution)/shard_map/ppermute | solution.py:143
  113.5 32.6 %collective-permute-start.5 = (bf16[16,8064]{1,0:T(8,128)(2,1)S(1)}, bf16[16,8064]{1,0:T(8,128)(2,1)S(1)}, u32[]{:S(2)}, u32[]{:S(2)}) collective-permute-start(bf16[16,8064]{1,0:T(8,128)(2,1)S(1)} %copy-done.21), channel_id=1, source_target_pairs={{0,6},{1,7},{2,4},{3,5},{4,2},{5,3},{6,0},{7,1},{8,14},{9,15},{10,... | collective-permute-start | bytes 774152 | tf_op jit(solution)/shard_map/ppermute | solution.py:143
  210.4 92.0 %collective-permute-start.31 = (bf16[16,8192]{1,0:T(8,128)(2,1)S(1)}, bf16[16,8192]{1,0:T(8,128)(2,1)S(1)}, u32[]{:S(2)}, u32[]{:S(2)}) collective-permute-start(bf16[16,8192]{1,0:T(8,128)(2,1)S(1)} %get-tuple-element.31), channel_id=1, source_target_pairs={{0,1},{1,0},{2,3},{3,2},{4,5},{5,4},{6,7},{7,6},{8,9},{9,8},{10,11... | collective-permute-start | bytes 786440 | tf_op jit(solution)/shard_map/ppermute | solution.py:143
  210.6 92.6 %collective-permute-start.32 = (bf16[16,8192]{1,0:T(8,128)(2,1)S(1)}, bf16[16,8192]{1,0:T(8,128)(2,1)S(1)}, u32[]{:S(2)}, u32[]{:S(2)}) collective-permute-start(bf16[16,8192]{1,0:T(8,128)(2,1)S(1)} %get-tuple-element.30), channel_id=1, source_target_pairs={{0,2},{1,3},{2,0},{3,1},{4,6},{5,7},{6,4},{7,5},{8,10},{9,11},{10,... | collective-permute-start | bytes 786440 | tf_op jit(solution)/shard_map/ppermute | solution.py:143
  210.6 93.5 %collective-permute-start.33 = (bf16[16,8192]{1,0:T(8,128)(2,1)S(1)}, bf16[16,8192]{1,0:T(8,128)(2,1)S(1)}, u32[]{:S(2)}, u32[]{:S(2)}) collective-permute-start(bf16[16,8192]{1,0:T(8,128)(2,1)S(1)} %get-tuple-element.29), channel_id=1, source_target_pairs={{0,3},{1,2},{2,1},{3,0},{4,7},{5,6},{6,5},{7,4},{8,11},{9,10},{10,... | collective-permute-start | bytes 786440 | tf_op jit(solution)/shard_map/ppermute | solution.py:143
  212.4 93.3 %collective-permute-start.34 = (bf16[16,8192]{1,0:T(8,128)(2,1)S(1)}, bf16[16,8192]{1,0:T(8,128)(2,1)S(1)}, u32[]{:S(2)}, u32[]{:S(2)}) collective-permute-start(bf16[16,8192]{1,0:T(8,128)(2,1)S(1)} %get-tuple-element.28), channel_id=1, source_target_pairs={{0,4},{1,5},{2,6},{3,7},{4,0},{5,1},{6,2},{7,3},{8,12},{9,13},{10,... | collective-permute-start | bytes 786440 | tf_op jit(solution)/shard_map/ppermute | solution.py:143
  302.5 24.7 %collective-permute-start.36 = (bf16[16,8192]{1,0:T(8,128)(2,1)S(1)}, bf16[16,8192]{1,0:T(8,128)(2,1)S(1)}, u32[]{:S(2)}, u32[]{:S(2)}) collective-permute-start(bf16[16,8192]{1,0:T(8,128)(2,1)S(1)} %get-tuple-element.26), channel_id=1, source_target_pairs={{0,6},{1,7},{2,4},{3,5},{4,2},{5,3},{6,0},{7,1},{8,14},{9,15},{10,... | collective-permute-start | bytes 786440 | tf_op jit(solution)/shard_map/ppermute | solution.py:143
  303.2 28.5 %collective-permute-start.37 = (bf16[16,8192]{1,0:T(8,128)(2,1)S(1)}, bf16[16,8192]{1,0:T(8,128)(2,1)S(1)}, u32[]{:S(2)}, u32[]{:S(2)}) collective-permute-start(bf16[16,8192]{1,0:T(8,128)(2,1)S(1)} %get-tuple-element.25), channel_id=1, source_target_pairs={{0,7},{1,6},{2,5},{3,4},{4,3},{5,2},{6,1},{7,0},{8,15},{9,14},{10,... | collective-permute-start | bytes 786440 | tf_op jit(solution)/shard_map/ppermute | solution.py:143
  304.1 35.9 %collective-permute-start.16 = (bf16[1,128,3584]{2,1,0:T(8,128)(2,1)S(1)}, bf16[1,128,3584]{2,1,0:T(8,128)(2,1)S(1)}, u32[]{:S(2)}, u32[]{:S(2)}) collective-permute-start(bf16[1,128,3584]{2,1,0:T(8,128)(2,1)S(1)} %fusion.16), channel_id=1, source_target_pairs={{24,0},{0,8},{8,16},{16,24},{25,1},{1,9},{9,17},{17,25},{26,2},{2,... | collective-permute-start | bytes 2752520 | tf_op jit(solution)/shard_map/ppermute | solution.py:18
  339.5 23.6 %collective-permute-start.38 = (bf16[1,128,3584]{2,1,0:T(8,128)(2,1)S(1)}, bf16[1,128,3584]{2,1,0:T(8,128)(2,1)S(1)}, u32[]{:S(2)}, u32[]{:S(2)}) collective-permute-start(bf16[1,128,3584]{2,1,0:T(8,128)(2,1)S(1)} %fusion.51), channel_id=1, source_target_pairs={{8,0},{16,8},{24,16},{0,24},{9,1},{17,9},{25,17},{1,25},{10,2},{18... | collective-permute-start | bytes 2752520 | tf_op jit(solution)/shard_map/ppermute | solution.py:18
  (101 other events, 1516.7 us)

commit v3 on v2

--- a/solution.py
+++ b/solution.py
@@ -137,11 +137,17 @@
         return out
 
     def swap(self, packed):
-        got = [packed[:ROWS]]
-        for j in range(1, self.devices):
+        got = {0: packed[:ROWS]}
+        for j in sorted(range(1, self.devices), key=lambda j: (-(j >> 1).bit_length(), -(j & 1), -j)):
             route = [(i, i ^ j) for i in range(self.devices)]
-            got.append(lax.ppermute(packed[j * ROWS : (j + 1) * ROWS], "expert", route))
-        return jnp.concatenate(got, axis=0)
+            got[j] = lax.ppermute(packed[j * ROWS : (j + 1) * ROWS], "expert", route)
+        return [got[j] for j in range(self.devices)]
+
+
+def joined(blocks, after=()):
+    if len(after):
+        blocks = lax.optimization_barrier((list(blocks), list(after)))[0]
+    return jnp.concatenate(blocks, axis=0)
 
 
 def slots_of(choose, experts, capacity):
@@ -184,7 +190,7 @@
     masks_a = [plan.masks(where_a[:, k]) for k in range(top)]
     wide_a, inv_a, normed_a = normalize(fwd_acts[0], gain)
     spread_a = [sum(each) for each in zip(*masks_a)]
-    got_a = plan.unpack(plan.swap(plan.dispatch(spread_a, normed_a)))
+    got_a = plan.unpack(joined(plan.swap(plan.dispatch(spread_a, normed_a))))
     _, _, _, gate_a = gating(normed_a, table, choose_a)
 
     choose_b = bwd_experts[0]
@@ -193,20 +199,27 @@
     masks_b = [plan.masks(where_b[:, k]) for k in range(top)]
     wide_b, inv_b, normed_b = normalize(bwd_saved[0], gain)
     spread_b = [sum(each) for each in zip(*masks_b)]
-    got_x = plan.unpack(plan.swap(plan.dispatch(spread_b, normed_b)))
-    got_g = plan.unpack(plan.swap(plan.dispatch(spread_b, grads_b)))
+    blocks_x = plan.swap(plan.dispatch(spread_b, normed_b))
+    sent_g = plan.dispatch(spread_b, grads_b)
     onehot_b, picked_b, total_b, gate_b = gating(normed_b, table, choose_b)
 
     y = jnp.zeros((got_a.shape[0], width), jnp.float32)
     for up, down in zip(ups, downs):
         hidden = jax.nn.silu(jnp.dot(got_a, up, preferred_element_type=jnp.float32))
         y += jnp.dot(hidden.astype(jnp.bfloat16), down, preferred_element_type=jnp.float32)
-    back_a = plan.swap(plan.pack(y.astype(jnp.bfloat16)))
+    sent_a = plan.pack(y.astype(jnp.bfloat16))
+
+    sent_g, sent_a = lax.optimization_barrier((sent_g, sent_a))
+    blocks_g = plan.swap(sent_g)
+    got_x = plan.unpack(joined(blocks_x, [sent_a]))
+    pres = [jnp.dot(got_x, up, preferred_element_type=jnp.float32) for up in ups]
+    pres, sent_a = lax.optimization_barrier((pres, sent_a))
+    back_a = plan.swap(sent_a)
+    got_g = plan.unpack(joined(blocks_g, pres))
 
     dx = jnp.zeros((got_a.shape[0], width), jnp.float32)
     dgate_rows = jnp.zeros((got_a.shape[0],), jnp.float32)
-    for up, down in zip(ups, downs):
-        pre = jnp.dot(got_x, up, preferred_element_type=jnp.float32)
+    for pre, up, down in zip(pres, ups, downs):
         sigma = jax.nn.sigmoid(pre)
         hidden = (pre * sigma).astype(jnp.bfloat16).astype(jnp.float32)
         back = lax.dot_general(
@@ -215,9 +228,9 @@
         dgate_rows += jnp.sum(hidden * back, axis=1)
         dpre = (back * sigma * (1.0 + pre * (1.0 - sigma))).astype(jnp.bfloat16)
         dx += lax.dot_general(dpre, up, (((1,), (1,)), ((), ())), preferred_element_type=jnp.float32)
-    back_x = plan.swap(
-        jnp.concatenate([plan.pack(dx.astype(jnp.bfloat16)), plan.numbers(dgate_rows)], axis=1)
-    )
+    sent_x = jnp.concatenate([plan.pack(dx.astype(jnp.bfloat16)), plan.numbers(dgate_rows)], axis=1)
+    back_x = joined(plan.swap(sent_x))
+    back_a = joined(back_a, [sent_x])
 
     out_a = wide_a
     for k in range(top):

time: 366 us -> 324 us (0.89)
  waiting for transfers between devices: 217 us -> 177 us
  matrix products: 73.5 us -> 64.9 us
  other arithmetic: 8.35 us -> 12.5 us
    ppermute x35, waiting for transfers between devices: 194 us -> 154 us  [swap(): got[j] = lax.ppermute(packed[j * ROWS:(j + 1) * ROWS], 'expert', route)]
    unnamed x206 -> x127, local copies, waits for them, and re-layouts: 15.5 us -> 20.3 us
  transfers between devices with their start and end apart: 39 -> 39, of which waited for: 22 -> 20; matrix products, arithmetic and copies ran while one was open for 20% -> 26% of each run, Pallas kernels for 0% -> 0%
where the time goes in v3:
time: 324 us; the launch traced here: 323 us
  waiting for transfers between devices  177 us (55%)
  matrix products  64.9 us (20%)
  local copies, waits for them, and re-layouts  33.4 us (10%)
  starting transfers between devices  32.9 us (10%)
  other arithmetic  12.5 us (4%)
    ppermute x35, waiting for transfers between devices, swap(): got[j] = lax.ppermute(packed[j * ROWS:(j + 1) * ROWS], 'expert', route)  154 us
    ppermute x35, starting transfers between devices, swap(): got[j] = lax.ppermute(packed[j * ROWS:(j + 1) * ROWS], 'expert', route)  30.2 us
    ppermute x2, waiting for transfers between devices, passed_along(): return lax.ppermute(block, axis, route)  23.1 us
    unnamed x127, local copies, waits for them, and re-layouts  20.3 us
    dot_general x2, matrix products, on_device(): jnp.dot(hidden.astype(jnp.bfloat16), down, preferred_element_type=jnp.flo...  16.8 us
    dot_general x32, matrix products, back_to_tokens(): lax.dot_general(mask, rows, (((0,), (0,)), ((), ())), preferred_element_t...  16.7 us
    dot_general x21, matrix products, pick(): jnp.dot(mask, rows, preferred_element_type=jnp.float32).astype(jnp.bfloat16)  9.81 us
    dot_general x2, matrix products, on_device(): lax.dot_general(dpre, up, (((1,), (1,)), ((), ())), preferred_element_typ...  6.8 us
  transfers between devices with their start and end apart: 39, of which 20 were waited for; matrix products, arithmetic and copies ran while one was open for 26% of the time, Pallas kernels for 0%

profile of v3, /device:TPU:10, one launch (start us, length us, event | category | flops | bytes accessed | tf_op | source)
XLA Modules:
  0.0 322.9 jit_solution(14097567640170178342)
XLA Ops:
  37.3 11.5 %collective-permute-done.11 = bf16[16,8064]{1,0:T(8,128)(2,1)} collective-permute-done((bf16[16,8064]{1,0:T(8,128)(2,1)}, bf16[16,8064]{1,0:T(8,128)(2,1)}, u32[]{:S(2)}, u32[]{:S(2)}) %collective-permute-start.11) | collective-permute-done | bytes 258080 | tf_op jit(solution)/shard_map/ppermute | solution.py:143
  49.7 4.4 %collective-permute-done.12 = bf16[16,8064]{1,0:T(8,128)(2,1)S(1)} collective-permute-done((bf16[16,8064]{1,0:T(8,128)(2,1)S(1)}, bf16[16,8064]{1,0:T(8,128)(2,1)S(1)}, u32[]{:S(2)}, u32[]{:S(2)}) %collective-permute-start.12) | collective-permute-done | bytes 258080 | tf_op jit(solution)/shard_map/ppermute | solution.py:143
  54.2 4.9 %collective-permute-done.13 = bf16[16,8064]{1,0:T(8,128)(2,1)S(1)} collective-permute-done((bf16[16,8064]{1,0:T(8,128)(2,1)S(1)}, bf16[16,8064]{1,0:T(8,128)(2,1)S(1)}, u32[]{:S(2)}, u32[]{:S(2)}) %collective-permute-start.13) | collective-permute-done | bytes 258080 | tf_op jit(solution)/shard_map/ppermute | solution.py:143
  61.9 8.1 %fusion.91 = f32[288,3584]{1,0:T(8,128)} fusion(bf16[1,512,3584]{2,1,0:T(8,128)(2,1)} %param.15, bf16[1,3584,512]{2,1,0:T(8,128)(2,1)} %param.14, bf16[32,896]{1,0:T(8,128)(2,1)S(1)} %convolution_convert_fusion.17, bf16[32,896]{1,0:T(8,128)(2,1)S(1)} %convolution_convert_fusion.18, bf16[32,896]{1,0:T(8,128)(2,1)S(1)} %convolution_convert_fusion.19, ...), kind=kOutput, calls=%fused_computation.148 | convolution fusion | flops 2127052800 | bytes 13533184 | tf_op jit(solution)/shard_map/dot_general | solution.py:209
  70.0 3.8 %collective-permute-start.3 = (bf16[16,8064]{1,0:T(8,128)(2,1)}, bf16[16,8064]{1,0:T(8,128)(2,1)}, u32[]{:S(2)}, u32[]{:S(2)}) collective-permute-start(bf16[16,8064]{1,0:T(8,128)(2,1)} %get-tuple-element.128), channel_id=1, source_target_pairs={{0,4},{1,5},{2,6},{3,7},{4,0},{5,1},{6,2},{7,3},{8,12},{9,13},{10,... | collective-permute-start | bytes 774152 | tf_op jit(solution)/shard_map/ppermute | solution.py:143
  73.8 8.7 %fusion = bf16[288,3584]{1,0:T(8,128)(2,1)} fusion(f32[288,3584]{1,0:T(8,128)} %fusion.91, bf16[512,3584]{1,0:T(8,128)(2,1)} %collective-permute-done.15, bf16[3584,512]{1,0:T(8,128)(2,1)} %collective-permute-done.14, bf16[32,896]{1,0:T(8,128)(2,1)S(1)} %convolution_convert_fusion.17, bf16[32,896]{1,0:T(8,128)(2,1)S(1)} %convolution_convert_fusion.18, ...), kind=kOutput, calls=%fused_computation.2 | convolution fusion | flops 2129117184 | bytes 15597568 | tf_op jit(solution)/shard_map/dot_general | solution.py:209
  90.8 16.6 %collective-permute-done.4 = bf16[16,8064]{1,0:T(8,128)(2,1)} collective-permute-done((bf16[16,8064]{1,0:T(8,128)(2,1)}, bf16[16,8064]{1,0:T(8,128)(2,1)}, u32[]{:S(2)}, u32[]{:S(2)}) %collective-permute-start.4) | collective-permute-done | bytes 258080 | tf_op jit(solution)/shard_map/ppermute | solution.py:143
  107.4 6.0 %collective-permute-done.5 = bf16[16,8064]{1,0:T(8,128)(2,1)S(1)} collective-permute-done((bf16[16,8064]{1,0:T(8,128)(2,1)S(1)}, bf16[16,8064]{1,0:T(8,128)(2,1)S(1)}, u32[]{:S(2)}, u32[]{:S(2)}) %collective-permute-start.5) | collective-permute-done | bytes 258080 | tf_op jit(solution)/shard_map/ppermute | solution.py:143
  113.3 5.2 %collective-permute-done.6 = bf16[16,8064]{1,0:T(8,128)(2,1)S(1)} collective-permute-done((bf16[16,8064]{1,0:T(8,128)(2,1)S(1)}, bf16[16,8064]{1,0:T(8,128)(2,1)S(1)}, u32[]{:S(2)}, u32[]{:S(2)}) %collective-permute-start.6) | collective-permute-done | bytes 258080 | tf_op jit(solution)/shard_map/ppermute | solution.py:143
  139.3 5.7 %collective-permute-done.25 = bf16[16,8064]{1,0:T(8,128)(2,1)S(1)} collective-permute-done((bf16[16,8064]{1,0:T(8,128)(2,1)S(1)}, bf16[16,8064]{1,0:T(8,128)(2,1)S(1)}, u32[]{:S(2)}, u32[]{:S(2)}) %collective-permute-start.25) | collective-permute-done | bytes 258080 | tf_op jit(solution)/shard_map/ppermute | solution.py:143
  145.1 18.9 %collective-permute-done.26 = bf16[16,8064]{1,0:T(8,128)(2,1)S(1)} collective-permute-done((bf16[16,8064]{1,0:T(8,128)(2,1)S(1)}, bf16[16,8064]{1,0:T(8,128)(2,1)S(1)}, u32[]{:S(2)}, u32[]{:S(2)}) %collective-permute-start.26) | collective-permute-done | bytes 258080 | tf_op jit(solution)/shard_map/ppermute | solution.py:143
  166.2 3.4 %collective-permute-done.27 = bf16[16,8064]{1,0:T(8,128)(2,1)S(1)} collective-permute-done((bf16[16,8064]{1,0:T(8,128)(2,1)S(1)}, bf16[16,8064]{1,0:T(8,128)(2,1)S(1)}, u32[]{:S(2)}, u32[]{:S(2)}) %collective-permute-start.27) | collective-permute-done | bytes 258080 | tf_op jit(solution)/shard_map/ppermute | solution.py:143
  171.2 4.6 %collective-permute-done.28 = bf16[16,8064]{1,0:T(8,128)(2,1)S(1)} collective-permute-done((bf16[16,8064]{1,0:T(8,128)(2,1)S(1)}, bf16[16,8064]{1,0:T(8,128)(2,1)S(1)}, u32[]{:S(2)}, u32[]{:S(2)}) %collective-permute-start.28) | collective-permute-done | bytes 258080 | tf_op jit(solution)/shard_map/ppermute | solution.py:143
  175.8 10.5 %collective-permute-done.29 = bf16[16,8064]{1,0:T(8,128)(2,1)S(1)} collective-permute-done((bf16[16,8064]{1,0:T(8,128)(2,1)S(1)}, bf16[16,8064]{1,0:T(8,128)(2,1)S(1)}, u32[]{:S(2)}, u32[]{:S(2)}) %collective-permute-start.29) | collective-permute-done | bytes 258080 | tf_op jit(solution)/shard_map/ppermute | solution.py:143
  193.4 3.4 %multiply_reduce_fusion = (f32[288]{0:T(512)S(1)}, f32[288,512]{1,0:T(8,128)S(1)}) fusion(f32[288,512]{1,0:T(8,128)S(1)} %fusion.327, bf16[512,3584]{1,0:T(8,128)(2,1)} %collective-permute-done.15, bf16[32,896]{1,0:T(8,128)(2,1)S(1)} %convolution_convert_fusion.9, bf16[32,896]{1,0:T(8,128)(2,1)S(1)} %convolution_convert_fusion.10, ...), kind=kOutput, calls=%fused_computation.138 | convolution fusion | flops 1070530304 | bytes 6915200 | tf_op jit(solution)/shard_map/dot_general | solution.py:225
  196.8 3.4 %fusion.1 = bf16[288,3584]{1,0:T(8,128)(2,1)S(1)} fusion(f32[288,3584]{1,0:T(8,128)S(1)} %fusion.92, bf16[3584,512]{1,0:T(8,128)(2,1)} %collective-permute-done.14, f32[288,512]{1,0:T(8,128)S(1)} %fusion.327, f32[288,512]{1,0:T(8,128)S(1)} %get-tuple-element.176), kind=kOutput, calls=%fused_computation.3 | convolution fusion | flops 1060356096 | bytes 11042816 | tf_op jit(solution)/shard_map/dot_general | solution.py:230
  209.0 18.0 %collective-permute-done.21 = bf16[16,8064]{1,0:T(8,128)(2,1)S(1)} collective-permute-done((bf16[16,8064]{1,0:T(8,128)(2,1)S(1)}, bf16[16,8064]{1,0:T(8,128)(2,1)S(1)}, u32[]{:S(2)}, u32[]{:S(2)}) %collective-permute-start.21) | collective-permute-done | bytes 258080 | tf_op jit(solution)/shard_map/ppermute | solution.py:143
  227.0 4.7 %collective-permute-done.22 = bf16[16,8064]{1,0:T(8,128)(2,1)S(1)} collective-permute-done((bf16[16,8064]{1,0:T(8,128)(2,1)S(1)}, bf16[16,8064]{1,0:T(8,128)(2,1)S(1)}, u32[]{:S(2)}, u32[]{:S(2)}) %collective-permute-start.22) | collective-permute-done | bytes 258080 | tf_op jit(solution)/shard_map/ppermute | solution.py:143
  248.2 9.9 %collective-permute-done.32 = bf16[16,8192]{1,0:T(8,128)(2,1)S(1)} collective-permute-done((bf16[16,8192]{1,0:T(8,128)(2,1)S(1)}, bf16[16,8192]{1,0:T(8,128)(2,1)S(1)}, u32[]{:S(2)}, u32[]{:S(2)}) %collective-permute-start.32) | collective-permute-done | bytes 262176 | tf_op jit(solution)/shard_map/ppermute | solution.py:143
  258.1 5.2 %collective-permute-done.33 = bf16[16,8192]{1,0:T(8,128)(2,1)S(1)} collective-permute-done((bf16[16,8192]{1,0:T(8,128)(2,1)S(1)}, bf16[16,8192]{1,0:T(8,128)(2,1)S(1)}, u32[]{:S(2)}, u32[]{:S(2)}) %collective-permute-start.33) | collective-permute-done | bytes 262176 | tf_op jit(solution)/shard_map/ppermute | solution.py:143
  264.9 13.6 %collective-permute-done.35 = bf16[16,8192]{1,0:T(8,128)(2,1)S(1)} collective-permute-done((bf16[16,8192]{1,0:T(8,128)(2,1)S(1)}, bf16[16,8192]{1,0:T(8,128)(2,1)S(1)}, u32[]{:S(2)}, u32[]{:S(2)}) %collective-permute-start.35) | collective-permute-done | bytes 262176 | tf_op jit(solution)/shard_map/ppermute | solution.py:143
  278.5 6.6 %collective-permute-done.36 = bf16[16,8192]{1,0:T(8,128)(2,1)S(1)} collective-permute-done((bf16[16,8192]{1,0:T(8,128)(2,1)S(1)}, bf16[16,8192]{1,0:T(8,128)(2,1)S(1)}, u32[]{:S(2)}, u32[]{:S(2)}) %collective-permute-start.36) | collective-permute-done | bytes 262176 | tf_op jit(solution)/shard_map/ppermute | solution.py:143
  285.1 4.4 %collective-permute-done.37 = bf16[16,8192]{1,0:T(8,128)(2,1)S(1)} collective-permute-done((bf16[16,8192]{1,0:T(8,128)(2,1)S(1)}, bf16[16,8192]{1,0:T(8,128)(2,1)S(1)}, u32[]{:S(2)}, u32[]{:S(2)}) %collective-permute-start.37) | collective-permute-done | bytes 262176 | tf_op jit(solution)/shard_map/ppermute | solution.py:143
  298.0 23.1 %collective-permute-done.38 = bf16[1,128,3584]{2,1,0:T(8,128)(2,1)S(1)} collective-permute-done((bf16[1,128,3584]{2,1,0:T(8,128)(2,1)S(1)}, bf16[1,128,3584]{2,1,0:T(8,128)(2,1)S(1)}, u32[]{:S(2)}, u32[]{:S(2)}) %collective-permute-start.38) | collective-permute-done | bytes 917536 | tf_op jit(solution)/shard_map/ppermute | solution.py:18
  (317 shorter events, 116.3 us)
Async XLA Ops:
  10.2 24.5 %collective-permute-start.9 = (bf16[16,8064]{1,0:T(8,128)(2,1)}, bf16[16,8064]{1,0:T(8,128)(2,1)}, u32[]{:S(2)}, u32[]{:S(2)}) collective-permute-start(bf16[16,8064]{1,0:T(8,128)(2,1)} %get-tuple-element.121), channel_id=1, source_target_pairs={{0,3},{1,2},{2,1},{3,0},{4,7},{5,6},{6,5},{7,4},{8,11},{9,10},{10,... | collective-permute-start | bytes 774152 | tf_op jit(solution)/shard_map/ppermute | solution.py:143
  11.6 24.4 %collective-permute-start.10 = (bf16[16,8064]{1,0:T(8,128)(2,1)}, bf16[16,8064]{1,0:T(8,128)(2,1)}, u32[]{:S(2)}, u32[]{:S(2)}) collective-permute-start(bf16[16,8064]{1,0:T(8,128)(2,1)} %get-tuple-element.120), channel_id=1, source_target_pairs={{0,4},{1,5},{2,6},{3,7},{4,0},{5,1},{6,2},{7,3},{8,12},{9,13},{10,... | collective-permute-start | bytes 774152 | tf_op jit(solution)/shard_map/ppermute | solution.py:143
  14.2 34.6 %collective-permute-start.11 = (bf16[16,8064]{1,0:T(8,128)(2,1)}, bf16[16,8064]{1,0:T(8,128)(2,1)}, u32[]{:S(2)}, u32[]{:S(2)}) collective-permute-start(bf16[16,8064]{1,0:T(8,128)(2,1)} %get-tuple-element.119), channel_id=1, source_target_pairs={{0,5},{1,4},{2,7},{3,6},{4,1},{5,0},{6,3},{7,2},{8,13},{9,12},{10,... | collective-permute-start | bytes 774152 | tf_op jit(solution)/shard_map/ppermute | solution.py:143
  33.2 25.9 %collective-permute-start.13 = (bf16[16,8064]{1,0:T(8,128)(2,1)S(1)}, bf16[16,8064]{1,0:T(8,128)(2,1)S(1)}, u32[]{:S(2)}, u32[]{:S(2)}) collective-permute-start(bf16[16,8064]{1,0:T(8,128)(2,1)S(1)} %copy-done.10), channel_id=1, source_target_pairs={{0,7},{1,6},{2,5},{3,4},{4,3},{5,2},{6,1},{7,0},{8,15},{9,14},{10,... | collective-permute-start | bytes 774152 | tf_op jit(solution)/shard_map/ppermute | solution.py:143
  34.7 35.4 %collective-permute-start.14 = (bf16[3584,512]{1,0:T(8,128)(2,1)}, bf16[3584,512]{1,0:T(8,128)(2,1)}, u32[]{:S(2)}, u32[]{:S(2)}) collective-permute-start(bf16[3584,512]{1,0:T(8,128)(2,1)} %bitcast.8), channel_id=1, source_target_pairs={{0,1},{1,0},{2,3},{3,2},{4,5},{5,4},{6,7},{7,6},{8,9},{9,8},{10,11... | collective-permute-start | bytes 11010056 | tf_op jit(solution)/shard_map/ppermute | solution.py:12
  35.9 37.9 %collective-permute-start.15 = (bf16[512,3584]{1,0:T(8,128)(2,1)}, bf16[512,3584]{1,0:T(8,128)(2,1)}, u32[]{:S(2)}, u32[]{:S(2)}) collective-permute-start(bf16[512,3584]{1,0:T(8,128)(2,1)} %bitcast.116), channel_id=1, source_target_pairs={{0,1},{1,0},{2,3},{3,2},{4,5},{5,4},{6,7},{7,6},{8,9},{9,8},{10,11... | collective-permute-start | bytes 11010056 | tf_op jit(solution)/shard_map/ppermute | solution.py:12
  48.7 40.2 %collective-permute-start = (bf16[16,8064]{1,0:T(8,128)(2,1)}, bf16[16,8064]{1,0:T(8,128)(2,1)}, u32[]{:S(2)}, u32[]{:S(2)}) collective-permute-start(bf16[16,8064]{1,0:T(8,128)(2,1)} %get-tuple-element.131), channel_id=1, source_target_pairs={{0,1},{1,0},{2,3},{3,2},{4,5},{5,4},{6,7},{7,6},{8,9},{9,8},{10,11... | collective-permute-start | bytes 774152 | tf_op jit(solution)/shard_map/ppermute | solution.py:143
  54.2 36.1 %collective-permute-start.1 = (bf16[16,8064]{1,0:T(8,128)(2,1)}, bf16[16,8064]{1,0:T(8,128)(2,1)}, u32[]{:S(2)}, u32[]{:S(2)}) collective-permute-start(bf16[16,8064]{1,0:T(8,128)(2,1)} %get-tuple-element.130), channel_id=1, source_target_pairs={{0,2},{1,3},{2,0},{3,1},{4,6},{5,7},{6,4},{7,5},{8,10},{9,11},{10,... | collective-permute-start | bytes 774152 | tf_op jit(solution)/shard_map/ppermute | solution.py:143
  59.0 31.7 %collective-permute-start.2 = (bf16[16,8064]{1,0:T(8,128)(2,1)}, bf16[16,8064]{1,0:T(8,128)(2,1)}, u32[]{:S(2)}, u32[]{:S(2)}) collective-permute-start(bf16[16,8064]{1,0:T(8,128)(2,1)} %get-tuple-element.129), channel_id=1, source_target_pairs={{0,3},{1,2},{2,1},{3,0},{4,7},{5,6},{6,5},{7,4},{8,11},{9,10},{10,... | collective-permute-start | bytes 774152 | tf_op jit(solution)/shard_map/ppermute | solution.py:143
  73.8 33.5 %collective-permute-start.4 = (bf16[16,8064]{1,0:T(8,128)(2,1)}, bf16[16,8064]{1,0:T(8,128)(2,1)}, u32[]{:S(2)}, u32[]{:S(2)}) collective-permute-start(bf16[16,8064]{1,0:T(8,128)(2,1)} %get-tuple-element.127), channel_id=1, source_target_pairs={{0,5},{1,4},{2,7},{3,6},{4,1},{5,0},{6,3},{7,2},{8,13},{9,12},{10,... | collective-permute-start | bytes 774152 | tf_op jit(solution)/shard_map/ppermute | solution.py:143
  89.0 24.4 %collective-permute-start.5 = (bf16[16,8064]{1,0:T(8,128)(2,1)S(1)}, bf16[16,8064]{1,0:T(8,128)(2,1)S(1)}, u32[]{:S(2)}, u32[]{:S(2)}) collective-permute-start(bf16[16,8064]{1,0:T(8,128)(2,1)S(1)} %copy-done.8), channel_id=1, source_target_pairs={{0,6},{1,7},{2,4},{3,5},{4,2},{5,3},{6,0},{7,1},{8,14},{9,15},{10,... | collective-permute-start | bytes 774152 | tf_op jit(solution)/shard_map/ppermute | solution.py:143
  90.2 28.3 %collective-permute-start.6 = (bf16[16,8064]{1,0:T(8,128)(2,1)S(1)}, bf16[16,8064]{1,0:T(8,128)(2,1)S(1)}, u32[]{:S(2)}, u32[]{:S(2)}) collective-permute-start(bf16[16,8064]{1,0:T(8,128)(2,1)S(1)} %get-tuple-element.125), channel_id=1, source_target_pairs={{0,7},{1,6},{2,5},{3,4},{4,3},{5,2},{6,1},{7,0},{8,15},{9,14},{10,... | collective-permute-start | bytes 774152 | tf_op jit(solution)/shard_map/ppermute | solution.py:143
  133.7 30.3 %collective-permute-start.26 = (bf16[16,8064]{1,0:T(8,128)(2,1)S(1)}, bf16[16,8064]{1,0:T(8,128)(2,1)S(1)}, u32[]{:S(2)}, u32[]{:S(2)}) collective-permute-start(bf16[16,8064]{1,0:T(8,128)(2,1)S(1)} %get-tuple-element.98), channel_id=1, source_target_pairs={{0,4},{1,5},{2,6},{3,7},{4,0},{5,1},{6,2},{7,3},{8,12},{9,13},{10,... | collective-permute-start | bytes 774152 | tf_op jit(solution)/shard_map/ppermute | solution.py:143
  135.3 34.3 %collective-permute-start.27 = (bf16[16,8064]{1,0:T(8,128)(2,1)S(1)}, bf16[16,8064]{1,0:T(8,128)(2,1)S(1)}, u32[]{:S(2)}, u32[]{:S(2)}) collective-permute-start(bf16[16,8064]{1,0:T(8,128)(2,1)S(1)} %get-tuple-element.97), channel_id=1, source_target_pairs={{0,5},{1,4},{2,7},{3,6},{4,1},{5,0},{6,3},{7,2},{8,13},{9,12},{10,... | collective-permute-start | bytes 774152 | tf_op jit(solution)/shard_map/ppermute | solution.py:143
  136.4 39.4 %collective-permute-start.28 = (bf16[16,8064]{1,0:T(8,128)(2,1)S(1)}, bf16[16,8064]{1,0:T(8,128)(2,1)S(1)}, u32[]{:S(2)}, u32[]{:S(2)}) collective-permute-start(bf16[16,8064]{1,0:T(8,128)(2,1)S(1)} %get-tuple-element.96), channel_id=1, source_target_pairs={{0,6},{1,7},{2,4},{3,5},{4,2},{5,3},{6,0},{7,1},{8,14},{9,15},{10,... | collective-permute-start | bytes 774152 | tf_op jit(solution)/shard_map/ppermute | solution.py:143
  138.1 48.1 %collective-permute-start.29 = (bf16[16,8064]{1,0:T(8,128)(2,1)S(1)}, bf16[16,8064]{1,0:T(8,128)(2,1)S(1)}, u32[]{:S(2)}, u32[]{:S(2)}) collective-permute-start(bf16[16,8064]{1,0:T(8,128)(2,1)S(1)} %get-tuple-element.95), channel_id=1, source_target_pairs={{0,7},{1,6},{2,5},{3,4},{4,3},{5,2},{6,1},{7,0},{8,15},{9,14},{10,... | collective-permute-start | bytes 774152 | tf_op jit(solution)/shard_map/ppermute | solution.py:143
  145.1 61.7 %collective-permute-start.16 = (bf16[16,8064]{1,0:T(8,128)(2,1)}, bf16[16,8064]{1,0:T(8,128)(2,1)}, u32[]{:S(2)}, u32[]{:S(2)}) collective-permute-start(bf16[16,8064]{1,0:T(8,128)(2,1)} %get-tuple-element.109), channel_id=1, source_target_pairs={{0,1},{1,0},{2,3},{3,2},{4,5},{5,4},{6,7},{7,6},{8,9},{9,8},{10,11... | collective-permute-start | bytes 774152 | tf_op jit(solution)/shard_map/ppermute | solution.py:143
  164.0 43.5 %collective-permute-start.17 = (bf16[16,8064]{1,0:T(8,128)(2,1)}, bf16[16,8064]{1,0:T(8,128)(2,1)}, u32[]{:S(2)}, u32[]{:S(2)}) collective-permute-start(bf16[16,8064]{1,0:T(8,128)(2,1)} %get-tuple-element.108), channel_id=1, source_target_pairs={{0,2},{1,3},{2,0},{3,1},{4,6},{5,7},{6,4},{7,5},{8,10},{9,11},{10,... | collective-permute-start | bytes 774152 | tf_op jit(solution)/shard_map/ppermute | solution.py:143
  169.6 39.4 %collective-permute-start.18 = (bf16[16,8064]{1,0:T(8,128)(2,1)}, bf16[16,8064]{1,0:T(8,128)(2,1)}, u32[]{:S(2)}, u32[]{:S(2)}) collective-permute-start(bf16[16,8064]{1,0:T(8,128)(2,1)} %get-tuple-element.107), channel_id=1, source_target_pairs={{0,3},{1,2},{2,1},{3,0},{4,7},{5,6},{6,5},{7,4},{8,11},{9,10},{10,... | collective-permute-start | bytes 774152 | tf_op jit(solution)/shard_map/ppermute | solution.py:143
  175.8 33.2 %collective-permute-start.19 = (bf16[16,8064]{1,0:T(8,128)(2,1)}, bf16[16,8064]{1,0:T(8,128)(2,1)}, u32[]{:S(2)}, u32[]{:S(2)}) collective-permute-start(bf16[16,8064]{1,0:T(8,128)(2,1)} %get-tuple-element.106), channel_id=1, source_target_pairs={{0,4},{1,5},{2,6},{3,7},{4,0},{5,1},{6,2},{7,3},{8,12},{9,13},{10,... | collective-permute-start | bytes 774152 | tf_op jit(solution)/shard_map/ppermute | solution.py:143
  243.7 34.8 %collective-permute-start.35 = (bf16[16,8192]{1,0:T(8,128)(2,1)S(1)}, bf16[16,8192]{1,0:T(8,128)(2,1)S(1)}, u32[]{:S(2)}, u32[]{:S(2)}) collective-permute-start(bf16[16,8192]{1,0:T(8,128)(2,1)S(1)} %get-tuple-element.85), channel_id=1, source_target_pairs={{0,5},{1,4},{2,7},{3,6},{4,1},{5,0},{6,3},{7,2},{8,13},{9,12},{10,... | collective-permute-start | bytes 786440 | tf_op jit(solution)/shard_map/ppermute | solution.py:143
  246.7 38.4 %collective-permute-start.36 = (bf16[16,8192]{1,0:T(8,128)(2,1)S(1)}, bf16[16,8192]{1,0:T(8,128)(2,1)S(1)}, u32[]{:S(2)}, u32[]{:S(2)}) collective-permute-start(bf16[16,8192]{1,0:T(8,128)(2,1)S(1)} %get-tuple-element.84), channel_id=1, source_target_pairs={{0,6},{1,7},{2,4},{3,5},{4,2},{5,3},{6,0},{7,1},{8,14},{9,15},{10,... | collective-permute-start | bytes 786440 | tf_op jit(solution)/shard_map/ppermute | solution.py:143
  258.1 31.5 %collective-permute-start.37 = (bf16[16,8192]{1,0:T(8,128)(2,1)S(1)}, bf16[16,8192]{1,0:T(8,128)(2,1)S(1)}, u32[]{:S(2)}, u32[]{:S(2)}) collective-permute-start(bf16[16,8192]{1,0:T(8,128)(2,1)S(1)} %get-tuple-element.83), channel_id=1, source_target_pairs={{0,7},{1,6},{2,5},{3,4},{4,3},{5,2},{6,1},{7,0},{8,15},{9,14},{10,... | collective-permute-start | bytes 786440 | tf_op jit(solution)/shard_map/ppermute | solution.py:143
  263.4 34.6 %collective-permute-start.30 = (bf16[1,128,3584]{2,1,0:T(8,128)(2,1)S(1)}, bf16[1,128,3584]{2,1,0:T(8,128)(2,1)S(1)}, u32[]{:S(2)}, u32[]{:S(2)}) collective-permute-start(bf16[1,128,3584]{2,1,0:T(8,128)(2,1)S(1)} %fusion.16), channel_id=1, source_target_pairs={{24,0},{0,8},{8,16},{16,24},{25,1},{1,9},{9,17},{17,25},{26,2},{2,... | collective-permute-start | bytes 2752520 | tf_op jit(solution)/shard_map/ppermute | solution.py:18
  (60 other events, 668.3 us)

commit v4 on v3

--- a/solution.py
+++ b/solution.py
@@ -39,9 +39,9 @@
 
 
 class Layout:
-    def __init__(self, width, half_cap, devices):
-        self.width, self.half_cap, self.devices = width, half_cap, devices
-        self.full, self.left = half_cap // ROWS, half_cap % ROWS
+    def __init__(self, width, capacity, pairs):
+        self.width, self.capacity, self.pairs = width, capacity, pairs
+        self.full, self.left = capacity // ROWS, capacity % ROWS
         self.pieces = ROWS // self.left if self.left else 1
         if self.left and (ROWS % self.left or width % (128 * self.pieces)):
             self.full, self.left, self.pieces = self.full + 1, 0, 1
@@ -49,13 +49,13 @@
         self.columns = self.full * width + (self.part if self.left else 0)
 
     def masks(self, where):
-        block = jnp.arange(self.devices * ROWS, dtype=jnp.int32)
-        to, row = lax.axis_index("expert") ^ (block // ROWS), block % ROWS
-        first = to * self.half_cap
+        block = jnp.arange(self.pairs * ROWS, dtype=jnp.int32)
+        to, row = lax.axis_index("expert") // HALVES ^ (block // ROWS), block % ROWS
+        first = to * self.capacity
         found = []
         for group in range(self.full):
             slot = group * ROWS + row
-            place = jnp.where(slot < self.half_cap, first + slot, -1)
+            place = jnp.where(slot < self.capacity, first + slot, -1)
             found.append((place[:, None] == where[None, :]).astype(jnp.bfloat16))
         for piece in range(self.pieces if self.left else 0):
             slot = self.full * ROWS + row % self.left
@@ -78,8 +78,8 @@
         return jnp.concatenate(cols, axis=1)
 
     def lifts(self):
-        slot = jnp.arange(self.devices * self.left, dtype=jnp.int32)
-        block = jnp.arange(self.devices * ROWS, dtype=jnp.int32)
+        slot = jnp.arange(self.pairs * self.left, dtype=jnp.int32)
+        block = jnp.arange(self.pairs * ROWS, dtype=jnp.int32)
         at = (slot // self.left) * ROWS + slot % self.left
         return [
             (at[:, None] + c * self.left == block[None, :]).astype(jnp.bfloat16)
@@ -94,7 +94,7 @@
         return jnp.concatenate(rows, axis=0)
 
     def pack(self, rows):
-        size = self.devices * ROWS
+        size = self.pairs * ROWS
         cols = [rows[g * size : (g + 1) * size] for g in range(self.full)]
         if self.left:
             tail = rows[self.full * size :]
@@ -106,7 +106,7 @@
         return jnp.concatenate(cols, axis=1)
 
     def numbers(self, values):
-        size = self.devices * ROWS
+        size = self.pairs * ROWS
         cols = [values[g * size : (g + 1) * size] for g in range(self.full)]
         if self.left:
             tail = values[self.full * size :]
@@ -138,10 +138,10 @@
 
     def swap(self, packed):
         got = {0: packed[:ROWS]}
-        for j in sorted(range(1, self.devices), key=lambda j: (-(j >> 1).bit_length(), -(j & 1), -j)):
-            route = [(i, i ^ j) for i in range(self.devices)]
+        for j in range(self.pairs - 1, 0, -1):
+            route = [(i, i ^ j * HALVES) for i in range(self.pairs * HALVES)]
             got[j] = lax.ppermute(packed[j * ROWS : (j + 1) * ROWS], "expert", route)
-        return [got[j] for j in range(self.devices)]
+        return [got[j] for j in range(self.pairs)]
 
 
 def joined(blocks, after=()):
@@ -179,9 +179,7 @@
     experts = table.shape[1]
     top = fwd_experts.shape[2]
     capacity = 9 * tok_rows * top // (8 * experts)
-    half_cap = capacity // HALVES
-    devices = lax.axis_size("expert")
-    plan = Layout(width, half_cap, devices)
+    plan = Layout(width, capacity, lax.axis_size("expert") // HALVES)
     ups = [w_up[0], partner(w_up[0], "expert", 0)]
     downs = [w_down[0], partner(w_down[0], "expert", 0)]
 

time: 324 us -> 289 us (0.89)
  waiting for transfers between devices: 177 us -> 155 us
  local copies, waits for them, and re-layouts: 33.4 us -> 28.1 us
  starting transfers between devices: 32.9 us -> 28.1 us
    ppermute x35 -> x15, waiting for transfers between devices: 154 us -> 137 us  [swap(): got[j] = lax.ppermute(packed[j * ROWS:(j + 1) * ROWS], 'expert', route)]
    unnamed x127 -> x107, local copies, waits for them, and re-layouts: 20.3 us -> 13.3 us
    ppermute x2, waiting for transfers between devices: 23.1 us -> 17.7 us  [passed_along(): return lax.ppermute(block, axis, route)]
    ppermute x35 -> x15, starting transfers between devices: 30.2 us -> 25.2 us  [swap(): got[j] = lax.ppermute(packed[j * ROWS:(j + 1) * ROWS], 'expert', route)]
    dot_general x32 -> x28, matrix products: 16.7 us -> 16.1 us  [back_to_tokens(): lax.dot_general(mask, rows, (((0,), (0,)), ((), ())), preferred_element_t...]
  transfers between devices with their start and end apart: 39 -> 19, of which waited for: 20 -> 10; matrix products, arithmetic and copies ran while one was open for 26% -> 25% of each run, Pallas kernels for 0% -> 0%
where the time goes in v4:
time: 289 us; the launch traced here: 287 us
  waiting for transfers between devices  155 us (54%)
  matrix products  64.3 us (22%)
  local copies, waits for them, and re-layouts  28.1 us (10%)
  starting transfers between devices  28.1 us (10%)
  other arithmetic  9.48 us (3%)
    ppermute x15, waiting for transfers between devices, swap(): got[j] = lax.ppermute(packed[j * ROWS:(j + 1) * ROWS], 'expert', route)  137 us
    ppermute x15, starting transfers between devices, swap(): got[j] = lax.ppermute(packed[j * ROWS:(j + 1) * ROWS], 'expert', route)  25.2 us
    ppermute x2, waiting for transfers between devices, passed_along(): return lax.ppermute(block, axis, route)  17.7 us
    dot_general x28, matrix products, back_to_tokens(): lax.dot_general(mask, rows, (((0,), (0,)), ((), ())), preferred_element_t...  16.1 us
    dot_general x2, matrix products, on_device(): jnp.dot(hidden.astype(jnp.bfloat16), down, preferred_element_type=jnp.flo...  15.6 us
    unnamed x107, local copies, waits for them, and re-layouts  13.3 us
    dot_general x21, matrix products, pick(): jnp.dot(mask, rows, preferred_element_type=jnp.float32).astype(jnp.bfloat16)  9.96 us
    dot_general x2, matrix products, on_device(): lax.dot_general(got_g, down, (((1,), (1,)), ((), ())), preferred_element_...  6.87 us
  transfers between devices with their start and end apart: 19, of which 10 were waited for; matrix products, arithmetic and copies ran while one was open for 25% of the time, Pallas kernels for 0%

profile of v4, /device:TPU:10, one launch (start us, length us, event | category | flops | bytes accessed | tf_op | source)
XLA Modules:
  0.0 286.8 jit_solution(17443000029611117313)
XLA Ops:
  10.1 2.6 collective-permute-start.4
  24.8 6.9 %collective-permute-done.3 = bf16[16,16128]{1,0:T(8,128)(2,1)} collective-permute-done((bf16[16,16128]{1,0:T(8,128)(2,1)}, bf16[16,16128]{1,0:T(8,128)(2,1)}, u32[]{:S(2)}, u32[]{:S(2)}) %collective-permute-start.3) | collective-permute-done | bytes 516128 | tf_op jit(solution)/shard_map/ppermute | solution.py:143
  31.7 2.5 collective-permute-start
  34.2 13.2 %collective-permute-done.4 = bf16[16,16128]{1,0:T(8,128)(2,1)} collective-permute-done((bf16[16,16128]{1,0:T(8,128)(2,1)}, bf16[16,16128]{1,0:T(8,128)(2,1)}, u32[]{:S(2)}, u32[]{:S(2)}) %collective-permute-start.4) | collective-permute-done | bytes 516128 | tf_op jit(solution)/shard_map/ppermute | solution.py:143
  47.4 3.4 %collective-permute-start.1 = (bf16[16,16128]{1,0:T(8,128)(2,1)}, bf16[16,16128]{1,0:T(8,128)(2,1)}, u32[]{:S(2)}, u32[]{:S(2)}) collective-permute-start(bf16[16,16128]{1,0:T(8,128)(2,1)} %get-tuple-element.96), channel_id=1, source_target_pairs={{0,4},{1,5},{2,6},{3,7},{4,0},{5,1},{6,2},{7,3},{8,12},{9,13},{10,... | collective-permute-start | bytes 1548296 | tf_op jit(solution)/shard_map/ppermute | solution.py:143
  50.8 30.7 %collective-permute-done.5 = bf16[16,16128]{1,0:T(8,128)(2,1)} collective-permute-done((bf16[16,16128]{1,0:T(8,128)(2,1)}, bf16[16,16128]{1,0:T(8,128)(2,1)}, u32[]{:S(2)}, u32[]{:S(2)}) %collective-permute-start.5) | collective-permute-done | bytes 516128 | tf_op jit(solution)/shard_map/ppermute | solution.py:143
  86.1 8.3 %fusion.110 = f32[288,3584]{1,0:T(8,128)} fusion(bf16[1,512,3584]{2,1,0:T(8,128)(2,1)} %param.15, bf16[288,3584]{1,0:T(8,128)(2,1)S(1)} %maximum_dynamic-update-slice_fusion, bf16[1,3584,512]{2,1,0:T(8,128)(2,1)} %param.14), kind=kOutput, calls=%fused_computation.181 | convolution fusion | flops 2114666496 | bytes 13533184 | tf_op jit(solution)/shard_map/dot_general | solution.py:207
  94.3 7.4 %fusion = bf16[288,3584]{1,0:T(8,128)(2,1)S(1)} fusion(f32[288,3584]{1,0:T(8,128)} %fusion.110, bf16[512,3584]{1,0:T(8,128)(2,1)} %collective-permute-done.7, bf16[288,3584]{1,0:T(8,128)(2,1)} %copy-done.8, bf16[3584,512]{1,0:T(8,128)(2,1)} %collective-permute-done.6), kind=kOutput, calls=%fused_computation.2 | convolution fusion | flops 2116730880 | bytes 15597568 | tf_op jit(solution)/shard_map/dot_general | solution.py:207
  106.7 3.4 %fusion.311 = f32[288,512]{1,0:T(8,128)S(1)} fusion(bf16[288,3584]{1,0:T(8,128)(2,1)S(1)} %maximum_dynamic-update-slice_fusion.1, bf16[1,3584,512]{2,1,0:T(8,128)(2,1)} %param.14), kind=kOutput, calls=%fused_computation.493 | convolution fusion | flops 1056964608 | bytes 6324224 | tf_op jit(solution)/shard_map/dot_general | solution.py:213
  110.2 3.3 %fusion.337 = f32[288,512]{1,0:T(8,128)S(1)} fusion(bf16[288,3584]{1,0:T(8,128)(2,1)S(1)} %maximum_dynamic-update-slice_fusion.1, bf16[3584,512]{1,0:T(8,128)(2,1)} %collective-permute-done.6), kind=kOutput, calls=%fused_computation.514 | convolution fusion | flops 1056964608 | bytes 6324224 | tf_op jit(solution)/shard_map/dot_general | solution.py:213
  115.2 2.4 collective-permute-start.12
  122.6 14.3 %collective-permute-done.11 = bf16[16,16128]{1,0:T(8,128)(2,1)S(1)} collective-permute-done((bf16[16,16128]{1,0:T(8,128)(2,1)S(1)}, bf16[16,16128]{1,0:T(8,128)(2,1)S(1)}, u32[]{:S(2)}, u32[]{:S(2)}) %collective-permute-start.11) | collective-permute-done | bytes 516128 | tf_op jit(solution)/shard_map/ppermute | solution.py:143
  136.9 4.4 %collective-permute-start.9 = (bf16[16,16128]{1,0:T(8,128)(2,1)}, bf16[16,16128]{1,0:T(8,128)(2,1)}, u32[]{:S(2)}, u32[]{:S(2)}) collective-permute-start(bf16[16,16128]{1,0:T(8,128)(2,1)} %get-tuple-element.88), channel_id=1, source_target_pairs={{0,4},{1,5},{2,6},{3,7},{4,0},{5,1},{6,2},{7,3},{8,12},{9,13},{10,... | collective-permute-start | bytes 1548296 | tf_op jit(solution)/shard_map/ppermute | solution.py:143
  141.3 21.6 %collective-permute-done.12 = bf16[16,16128]{1,0:T(8,128)(2,1)S(1)} collective-permute-done((bf16[16,16128]{1,0:T(8,128)(2,1)S(1)}, bf16[16,16128]{1,0:T(8,128)(2,1)S(1)}, u32[]{:S(2)}, u32[]{:S(2)}) %collective-permute-start.12) | collective-permute-done | bytes 516128 | tf_op jit(solution)/shard_map/ppermute | solution.py:143
  163.0 23.7 %collective-permute-done.13 = bf16[16,16128]{1,0:T(8,128)(2,1)S(1)} collective-permute-done((bf16[16,16128]{1,0:T(8,128)(2,1)S(1)}, bf16[16,16128]{1,0:T(8,128)(2,1)S(1)}, u32[]{:S(2)}, u32[]{:S(2)}) %collective-permute-start.13) | collective-permute-done | bytes 516128 | tf_op jit(solution)/shard_map/ppermute | solution.py:143
  187.5 3.4 %multiply_reduce_fusion.1 = (f32[288]{0:T(512)S(1)}, f32[288,512]{1,0:T(8,128)S(1)}) fusion(f32[288,512]{1,0:T(8,128)S(1)} %fusion.311, bf16[288,3584]{1,0:T(8,128)(2,1)S(1)} %maximum_dynamic-update-slice_fusion.2, bf16[1,512,3584]{2,1,0:T(8,128)(2,1)} %param.15), kind=kOutput, calls=%fused_computation.129 | convolution fusion | flops 1058144000 | bytes 6915200 | tf_op jit(solution)/shard_map/dot_general | solution.py:223
  190.9 3.4 %multiply_reduce_fusion = (f32[288]{0:T(512)S(1)}, f32[288,512]{1,0:T(8,128)S(1)}) fusion(f32[288,512]{1,0:T(8,128)S(1)} %fusion.337, bf16[288,3584]{1,0:T(8,128)(2,1)S(1)} %maximum_dynamic-update-slice_fusion.2, bf16[512,3584]{1,0:T(8,128)(2,1)} %collective-permute-done.7), kind=kOutput, calls=%fused_computation.127 | convolution fusion | flops 1058144000 | bytes 6915200 | tf_op jit(solution)/shard_map/dot_general | solution.py:223
  195.0 3.4 %fusion.111 = f32[288,3584]{1,0:T(8,128)S(1)} fusion(f32[288,512]{1,0:T(8,128)S(1)} %fusion.311, f32[288,512]{1,0:T(8,128)S(1)} %get-tuple-element.130, bf16[1,3584,512]{2,1,0:T(8,128)(2,1)} %param.14), kind=kOutput, calls=%fused_computation.182 | convolution fusion | flops 1058291712 | bytes 8978432 | tf_op jit(solution)/shard_map/dot_general | solution.py:228
  198.4 3.4 %fusion.1 = bf16[288,3584]{1,0:T(8,128)(2,1)S(1)} fusion(f32[288,3584]{1,0:T(8,128)S(1)} %fusion.111, bf16[3584,512]{1,0:T(8,128)(2,1)} %collective-permute-done.6, f32[288,512]{1,0:T(8,128)S(1)} %fusion.337, f32[288,512]{1,0:T(8,128)S(1)} %get-tuple-element.132), kind=kOutput, calls=%fused_computation.3 | convolution fusion | flops 1060356096 | bytes 11042816 | tf_op jit(solution)/shard_map/dot_general | solution.py:228
  220.5 2.4 collective-permute-start.16
  230.2 5.3 %collective-permute-done.15 = bf16[16,16256]{1,0:T(8,128)(2,1)S(1)} collective-permute-done((bf16[16,16256]{1,0:T(8,128)(2,1)S(1)}, bf16[16,16256]{1,0:T(8,128)(2,1)S(1)}, u32[]{:S(2)}, u32[]{:S(2)}) %collective-permute-start.15) | collective-permute-done | bytes 520224 | tf_op jit(solution)/shard_map/ppermute | solution.py:143
  235.5 13.5 %collective-permute-done.16 = bf16[16,16256]{1,0:T(8,128)(2,1)S(1)} collective-permute-done((bf16[16,16256]{1,0:T(8,128)(2,1)S(1)}, bf16[16,16256]{1,0:T(8,128)(2,1)S(1)}, u32[]{:S(2)}, u32[]{:S(2)}) %collective-permute-start.16) | collective-permute-done | bytes 520224 | tf_op jit(solution)/shard_map/ppermute | solution.py:143
  249.0 8.1 %collective-permute-done.17 = bf16[16,16256]{1,0:T(8,128)(2,1)S(1)} collective-permute-done((bf16[16,16256]{1,0:T(8,128)(2,1)S(1)}, bf16[16,16256]{1,0:T(8,128)(2,1)S(1)}, u32[]{:S(2)}, u32[]{:S(2)}) %collective-permute-start.17) | collective-permute-done | bytes 520224 | tf_op jit(solution)/shard_map/ppermute | solution.py:143
  267.3 17.7 %collective-permute-done.18 = bf16[1,128,3584]{2,1,0:T(8,128)(2,1)S(1)} collective-permute-done((bf16[1,128,3584]{2,1,0:T(8,128)(2,1)S(1)}, bf16[1,128,3584]{2,1,0:T(8,128)(2,1)S(1)}, u32[]{:S(2)}, u32[]{:S(2)}) %collective-permute-start.18) | collective-permute-done | bytes 917536 | tf_op jit(solution)/shard_map/ppermute | solution.py:18
  (248 shorter events, 76.4 us)
Async XLA Ops:
  0.7 19.3 %copy-start.18 = (s32[64]{0:T(128)}, s32[64]{0:T(128)S(1)}, u32[]{:S(2)}) copy-start(s32[64]{0:T(128)S(1)} %get-tuple-element.140) | copy-start | bytes 772
  0.7 19.7 %copy-start.16 = (s32[64]{0:T(128)}, s32[64]{0:T(128)S(1)}, u32[]{:S(2)}) copy-start(s32[64]{0:T(128)S(1)} %get-tuple-element.139) | copy-start | bytes 772
  9.7 22.1 %collective-permute-start.3 = (bf16[16,16128]{1,0:T(8,128)(2,1)}, bf16[16,16128]{1,0:T(8,128)(2,1)}, u32[]{:S(2)}, u32[]{:S(2)}) collective-permute-start(bf16[16,16128]{1,0:T(8,128)(2,1)} %get-tuple-element.94), channel_id=1, source_target_pairs={{0,2},{1,3},{2,0},{3,1},{4,6},{5,7},{6,4},{7,5},{8,10},{9,11},{10,... | collective-permute-start | bytes 1548296 | tf_op jit(solution)/shard_map/ppermute | solution.py:143
  10.1 37.3 %collective-permute-start.4 = (bf16[16,16128]{1,0:T(8,128)(2,1)}, bf16[16,16128]{1,0:T(8,128)(2,1)}, u32[]{:S(2)}, u32[]{:S(2)}) collective-permute-start(bf16[16,16128]{1,0:T(8,128)(2,1)} %get-tuple-element.93), channel_id=1, source_target_pairs={{0,4},{1,5},{2,6},{3,7},{4,0},{5,1},{6,2},{7,3},{8,12},{9,13},{10,... | collective-permute-start | bytes 1548296 | tf_op jit(solution)/shard_map/ppermute | solution.py:143
  12.7 68.8 %collective-permute-start.5 = (bf16[16,16128]{1,0:T(8,128)(2,1)}, bf16[16,16128]{1,0:T(8,128)(2,1)}, u32[]{:S(2)}, u32[]{:S(2)}) collective-permute-start(bf16[16,16128]{1,0:T(8,128)(2,1)} %get-tuple-element.92), channel_id=1, source_target_pairs={{0,6},{1,7},{2,4},{3,5},{4,2},{5,3},{6,0},{7,1},{8,14},{9,15},{10,... | collective-permute-start | bytes 1548296 | tf_op jit(solution)/shard_map/ppermute | solution.py:143
  13.2 81.2 %collective-permute-start.6 = (bf16[3584,512]{1,0:T(8,128)(2,1)}, bf16[3584,512]{1,0:T(8,128)(2,1)}, u32[]{:S(2)}, u32[]{:S(2)}) collective-permute-start(bf16[3584,512]{1,0:T(8,128)(2,1)} %bitcast.8), channel_id=1, source_target_pairs={{0,1},{1,0},{2,3},{3,2},{4,5},{5,4},{6,7},{7,6},{8,9},{9,8},{10,11... | collective-permute-start | bytes 11010056 | tf_op jit(solution)/shard_map/ppermute | solution.py:12
  13.2 81.2 %collective-permute-start.7 = (bf16[512,3584]{1,0:T(8,128)(2,1)}, bf16[512,3584]{1,0:T(8,128)(2,1)}, u32[]{:S(2)}, u32[]{:S(2)}) collective-permute-start(bf16[512,3584]{1,0:T(8,128)(2,1)} %bitcast.9), channel_id=1, source_target_pairs={{0,1},{1,0},{2,3},{3,2},{4,5},{5,4},{6,7},{7,6},{8,9},{9,8},{10,11... | collective-permute-start | bytes 11010056 | tf_op jit(solution)/shard_map/ppermute | solution.py:12
  13.7 173.2 %copy-start.25 = (s32[32]{0:T(128)}, s32[32]{0:T(128)S(1)}, u32[]{:S(2)}) copy-start(s32[32]{0:T(128)S(1)} %broadcast_add_fusion) | copy-start | bytes 388
  22.5 61.7 %copy-start.28 = (s32[128,2]{0,1:T(2,128)}, s32[128,2]{0,1:T(2,128)S(1)}, u32[]{:S(2)}) copy-start(s32[128,2]{0,1:T(2,128)S(1)} %copy.59) | copy-start | bytes 3076
  24.2 162.9 %copy-start.26 = (s32[32]{0:T(128)}, s32[32]{0:T(128)S(1)}, u32[]{:S(2)}) copy-start(s32[32]{0:T(128)S(1)} %fusion.298) | copy-start | bytes 388
  31.7 70.8 %collective-permute-start = (bf16[16,16128]{1,0:T(8,128)(2,1)}, bf16[16,16128]{1,0:T(8,128)(2,1)}, u32[]{:S(2)}, u32[]{:S(2)}) collective-permute-start(bf16[16,16128]{1,0:T(8,128)(2,1)} %get-tuple-element.97), channel_id=1, source_target_pairs={{0,2},{1,3},{2,0},{3,1},{4,6},{5,7},{6,4},{7,5},{8,10},{9,11},{10,... | collective-permute-start | bytes 1548296 | tf_op jit(solution)/shard_map/ppermute | solution.py:143
  47.4 55.2 %collective-permute-start.1 = (bf16[16,16128]{1,0:T(8,128)(2,1)}, bf16[16,16128]{1,0:T(8,128)(2,1)}, u32[]{:S(2)}, u32[]{:S(2)}) collective-permute-start(bf16[16,16128]{1,0:T(8,128)(2,1)} %get-tuple-element.96), channel_id=1, source_target_pairs={{0,4},{1,5},{2,6},{3,7},{4,0},{5,1},{6,2},{7,3},{8,12},{9,13},{10,... | collective-permute-start | bytes 1548296 | tf_op jit(solution)/shard_map/ppermute | solution.py:143
  81.5 21.1 %collective-permute-start.2 = (bf16[16,16128]{1,0:T(8,128)(2,1)}, bf16[16,16128]{1,0:T(8,128)(2,1)}, u32[]{:S(2)}, u32[]{:S(2)}) collective-permute-start(bf16[16,16128]{1,0:T(8,128)(2,1)} %get-tuple-element.95), channel_id=1, source_target_pairs={{0,6},{1,7},{2,4},{3,5},{4,2},{5,3},{6,0},{7,1},{8,14},{9,15},{10,... | collective-permute-start | bytes 1548296 | tf_op jit(solution)/shard_map/ppermute | solution.py:143
  115.1 21.9 %collective-permute-start.11 = (bf16[16,16128]{1,0:T(8,128)(2,1)S(1)}, bf16[16,16128]{1,0:T(8,128)(2,1)S(1)}, u32[]{:S(2)}, u32[]{:S(2)}) collective-permute-start(bf16[16,16128]{1,0:T(8,128)(2,1)S(1)} %get-tuple-element.85), channel_id=1, source_target_pairs={{0,2},{1,3},{2,0},{3,1},{4,6},{5,7},{6,4},{7,5},{8,10},{9,11},{10,... | collective-permute-start | bytes 1548296 | tf_op jit(solution)/shard_map/ppermute | solution.py:143
  115.2 47.8 %collective-permute-start.12 = (bf16[16,16128]{1,0:T(8,128)(2,1)S(1)}, bf16[16,16128]{1,0:T(8,128)(2,1)S(1)}, u32[]{:S(2)}, u32[]{:S(2)}) collective-permute-start(bf16[16,16128]{1,0:T(8,128)(2,1)S(1)} %get-tuple-element.84), channel_id=1, source_target_pairs={{0,4},{1,5},{2,6},{3,7},{4,0},{5,1},{6,2},{7,3},{8,12},{9,13},{10,... | collective-permute-start | bytes 1548296 | tf_op jit(solution)/shard_map/ppermute | solution.py:143
  117.5 69.1 %collective-permute-start.13 = (bf16[16,16128]{1,0:T(8,128)(2,1)S(1)}, bf16[16,16128]{1,0:T(8,128)(2,1)S(1)}, u32[]{:S(2)}, u32[]{:S(2)}) collective-permute-start(bf16[16,16128]{1,0:T(8,128)(2,1)S(1)} %get-tuple-element.83), channel_id=1, source_target_pairs={{0,6},{1,7},{2,4},{3,5},{4,2},{5,3},{6,0},{7,1},{8,14},{9,15},{10,... | collective-permute-start | bytes 1548296 | tf_op jit(solution)/shard_map/ppermute | solution.py:143
  119.8 95.0 %collective-permute-start.10 = (bf16[16,16128]{1,0:T(8,128)(2,1)}, bf16[16,16128]{1,0:T(8,128)(2,1)}, u32[]{:S(2)}, u32[]{:S(2)}) collective-permute-start(bf16[16,16128]{1,0:T(8,128)(2,1)} %get-tuple-element.87), channel_id=1, source_target_pairs={{0,6},{1,7},{2,4},{3,5},{4,2},{5,3},{6,0},{7,1},{8,14},{9,15},{10,... | collective-permute-start | bytes 1548296 | tf_op jit(solution)/shard_map/ppermute | solution.py:143
  120.8 94.1 %collective-permute-start.8 = (bf16[16,16128]{1,0:T(8,128)(2,1)}, bf16[16,16128]{1,0:T(8,128)(2,1)}, u32[]{:S(2)}, u32[]{:S(2)}) collective-permute-start(bf16[16,16128]{1,0:T(8,128)(2,1)} %get-tuple-element.89), channel_id=1, source_target_pairs={{0,2},{1,3},{2,0},{3,1},{4,6},{5,7},{6,4},{7,5},{8,10},{9,11},{10,... | collective-permute-start | bytes 1548296 | tf_op jit(solution)/shard_map/ppermute | solution.py:143
  136.9 77.9 %collective-permute-start.9 = (bf16[16,16128]{1,0:T(8,128)(2,1)}, bf16[16,16128]{1,0:T(8,128)(2,1)}, u32[]{:S(2)}, u32[]{:S(2)}) collective-permute-start(bf16[16,16128]{1,0:T(8,128)(2,1)} %get-tuple-element.88), channel_id=1, source_target_pairs={{0,4},{1,5},{2,6},{3,7},{4,0},{5,1},{6,2},{7,3},{8,12},{9,13},{10,... | collective-permute-start | bytes 1548296 | tf_op jit(solution)/shard_map/ppermute | solution.py:143
  220.4 15.1 %collective-permute-start.15 = (bf16[16,16256]{1,0:T(8,128)(2,1)S(1)}, bf16[16,16256]{1,0:T(8,128)(2,1)S(1)}, u32[]{:S(2)}, u32[]{:S(2)}) collective-permute-start(bf16[16,16256]{1,0:T(8,128)(2,1)S(1)} %get-tuple-element.82), channel_id=1, source_target_pairs={{0,2},{1,3},{2,0},{3,1},{4,6},{5,7},{6,4},{7,5},{8,10},{9,11},{10,... | collective-permute-start | bytes 1560584 | tf_op jit(solution)/shard_map/ppermute | solution.py:143
  220.5 28.5 %collective-permute-start.16 = (bf16[16,16256]{1,0:T(8,128)(2,1)S(1)}, bf16[16,16256]{1,0:T(8,128)(2,1)S(1)}, u32[]{:S(2)}, u32[]{:S(2)}) collective-permute-start(bf16[16,16256]{1,0:T(8,128)(2,1)S(1)} %get-tuple-element.81), channel_id=1, source_target_pairs={{0,4},{1,5},{2,6},{3,7},{4,0},{5,1},{6,2},{7,3},{8,12},{9,13},{10,... | collective-permute-start | bytes 1560584 | tf_op jit(solution)/shard_map/ppermute | solution.py:143
  222.9 34.2 %collective-permute-start.17 = (bf16[16,16256]{1,0:T(8,128)(2,1)S(1)}, bf16[16,16256]{1,0:T(8,128)(2,1)S(1)}, u32[]{:S(2)}, u32[]{:S(2)}) collective-permute-start(bf16[16,16256]{1,0:T(8,128)(2,1)S(1)} %get-tuple-element.80), channel_id=1, source_target_pairs={{0,6},{1,7},{2,4},{3,5},{4,2},{5,3},{6,0},{7,1},{8,14},{9,15},{10,... | collective-permute-start | bytes 1560584 | tf_op jit(solution)/shard_map/ppermute | solution.py:143
  228.4 38.8 %collective-permute-start.14 = (bf16[1,128,3584]{2,1,0:T(8,128)(2,1)S(1)}, bf16[1,128,3584]{2,1,0:T(8,128)(2,1)S(1)}, u32[]{:S(2)}, u32[]{:S(2)}) collective-permute-start(bf16[1,128,3584]{2,1,0:T(8,128)(2,1)S(1)} %fusion.20), channel_id=1, source_target_pairs={{24,0},{0,8},{8,16},{16,24},{25,1},{1,9},{9,17},{17,25},{26,2},{2,... | collective-permute-start | bytes 2752520 | tf_op jit(solution)/shard_map/ppermute | solution.py:18
  266.6 18.3 %collective-permute-start.18 = (bf16[1,128,3584]{2,1,0:T(8,128)(2,1)S(1)}, bf16[1,128,3584]{2,1,0:T(8,128)(2,1)S(1)}, u32[]{:S(2)}, u32[]{:S(2)}) collective-permute-start(bf16[1,128,3584]{2,1,0:T(8,128)(2,1)S(1)} %fusion.70), channel_id=1, source_target_pairs={{8,0},{16,8},{24,16},{0,24},{9,1},{17,9},{25,17},{1,25},{10,2},{18... | collective-permute-start | bytes 2752520 | tf_op jit(solution)/shard_map/ppermute | solution.py:18
  (32 other events, 134.6 us)

commit v5 on v4

--- a/solution.py
+++ b/solution.py
@@ -207,7 +207,6 @@
         y += jnp.dot(hidden.astype(jnp.bfloat16), down, preferred_element_type=jnp.float32)
     sent_a = plan.pack(y.astype(jnp.bfloat16))
 
-    sent_g, sent_a = lax.optimization_barrier((sent_g, sent_a))
     blocks_g = plan.swap(sent_g)
     got_x = plan.unpack(joined(blocks_x, [sent_a]))
     pres = [jnp.dot(got_x, up, preferred_element_type=jnp.float32) for up in ups]

time: 289 us -> 283 us (0.979)
  waiting for transfers between devices: 155 us -> 162 us
  matrix products: 64.3 us -> 59.6 us
  local copies, waits for them, and re-layouts: 28.1 us -> 24.2 us
    ppermute x2, waiting for transfers between devices: 17.7 us -> 22.1 us  [passed_along(): return lax.ppermute(block, axis, route)]
    unnamed x107 -> x121, local copies, waits for them, and re-layouts: 13.3 us -> 17.2 us
    dot_general x21, matrix products: 9.96 us -> 6.11 us  [pick(): jnp.dot(mask, rows, preferred_element_type=jnp.float32).astype(jnp.bfloat16)]
    ppermute x15, waiting for transfers between devices: 137 us -> 140 us  [swap(): got[j] = lax.ppermute(packed[j * ROWS:(j + 1) * ROWS], 'expert', route)]
  transfers between devices with their start and end apart: 19 -> 19, of which waited for: 10 -> 10; matrix products, arithmetic and copies ran while one was open for 25% -> 21% of each run, Pallas kernels for 0% -> 0%
where the time goes in v5:
time: 283 us; the launch traced here: 282 us
  waiting for transfers between devices  162 us (57%)
  matrix products  59.6 us (21%)
  starting transfers between devices  25.6 us (9%)
  local copies, waits for them, and re-layouts  24.2 us (9%)
  other arithmetic  8.65 us (3%)
    ppermute x15, waiting for transfers between devices, swap(): got[j] = lax.ppermute(packed[j * ROWS:(j + 1) * ROWS], 'expert', route)  140 us
    ppermute x15, starting transfers between devices, swap(): got[j] = lax.ppermute(packed[j * ROWS:(j + 1) * ROWS], 'expert', route)  22.7 us
    ppermute x2, waiting for transfers between devices, passed_along(): return lax.ppermute(block, axis, route)  22.1 us
    unnamed x121, local copies, waits for them, and re-layouts  17.2 us
    dot_general x2, matrix products, on_device(): jnp.dot(hidden.astype(jnp.bfloat16), down, preferred_element_type=jnp.flo...  15.5 us
    dot_general x28, matrix products, back_to_tokens(): lax.dot_general(mask, rows, (((0,), (0,)), ((), ())), preferred_element_t...  14.2 us
    dot_general x2, matrix products, on_device(): lax.dot_general(got_g, down, (((1,), (1,)), ((), ())), preferred_element_...  6.88 us
    dot_general x2, matrix products, on_device(): lax.dot_general(dpre, up, (((1,), (1,)), ((), ())), preferred_element_typ...  6.82 us
  transfers between devices with their start and end apart: 19, of which 10 were waited for; matrix products, arithmetic and copies ran while one was open for 21% of the time, Pallas kernels for 0%

profile of v5, /device:TPU:10, one launch (start us, length us, event | category | flops | bytes accessed | tf_op | source)
XLA Modules:
  0.0 282.4 jit_solution(12013835372182027353)
XLA Ops:
  10.2 2.6 collective-permute-start.4
  24.0 7.8 %collective-permute-done.3 = bf16[16,16128]{1,0:T(8,128)(2,1)S(1)} collective-permute-done((bf16[16,16128]{1,0:T(8,128)(2,1)}, bf16[16,16128]{1,0:T(8,128)(2,1)S(1)}, u32[]{:S(2)}, u32[]{:S(2)}) %collective-permute-start.3) | collective-permute-done | bytes 516128 | tf_op jit(solution)/shard_map/ppermute | solution.py:143
  31.8 2.4 collective-permute-start
  34.1 13.3 %collective-permute-done.4 = bf16[16,16128]{1,0:T(8,128)(2,1)} collective-permute-done((bf16[16,16128]{1,0:T(8,128)(2,1)}, bf16[16,16128]{1,0:T(8,128)(2,1)}, u32[]{:S(2)}, u32[]{:S(2)}) %collective-permute-start.4) | collective-permute-done | bytes 516128 | tf_op jit(solution)/shard_map/ppermute | solution.py:143
  47.4 3.4 %collective-permute-start.1 = (bf16[16,16128]{1,0:T(8,128)(2,1)}, bf16[16,16128]{1,0:T(8,128)(2,1)}, u32[]{:S(2)}, u32[]{:S(2)}) collective-permute-start(bf16[16,16128]{1,0:T(8,128)(2,1)} %get-tuple-element.92), channel_id=1, source_target_pairs={{0,4},{1,5},{2,6},{3,7},{4,0},{5,1},{6,2},{7,3},{8,12},{9,13},{10,... | collective-permute-start | bytes 1548296 | tf_op jit(solution)/shard_map/ppermute | solution.py:143
  50.8 30.7 %collective-permute-done.5 = bf16[16,16128]{1,0:T(8,128)(2,1)} collective-permute-done((bf16[16,16128]{1,0:T(8,128)(2,1)}, bf16[16,16128]{1,0:T(8,128)(2,1)}, u32[]{:S(2)}, u32[]{:S(2)}) %collective-permute-start.5) | collective-permute-done | bytes 516128 | tf_op jit(solution)/shard_map/ppermute | solution.py:143
  89.7 8.1 %fusion.110 = f32[288,3584]{1,0:T(8,128)} fusion(bf16[1,512,3584]{2,1,0:T(8,128)(2,1)} %param.15, bf16[288,3584]{1,0:T(8,128)(2,1)} %maximum_dynamic-update-slice_fusion, bf16[1,3584,512]{2,1,0:T(8,128)(2,1)} %param.14), kind=kOutput, calls=%fused_computation.181 | convolution fusion | flops 2114666496 | bytes 13533184 | tf_op jit(solution)/shard_map/dot_general | solution.py:207
  97.9 1.9 collective-permute-start.12
  99.8 7.4 %fusion = bf16[288,3584]{1,0:T(8,128)(2,1)S(1)} fusion(f32[288,3584]{1,0:T(8,128)} %fusion.110, bf16[512,3584]{1,0:T(8,128)(2,1)} %collective-permute-done.7, bf16[288,3584]{1,0:T(8,128)(2,1)} %maximum_dynamic-update-slice_fusion, bf16[3584,512]{1,0:T(8,128)(2,1)} %collective-permute-done.6), kind=kOutput, calls=%fused_computation.2 | convolution fusion | flops 2116730880 | bytes 15597568 | tf_op jit(solution)/shard_map/dot_general | solution.py:207
  110.1 15.7 %collective-permute-done.2 = bf16[16,16128]{1,0:T(8,128)(2,1)} collective-permute-done((bf16[16,16128]{1,0:T(8,128)(2,1)}, bf16[16,16128]{1,0:T(8,128)(2,1)}, u32[]{:S(2)}, u32[]{:S(2)}) %collective-permute-start.2) | collective-permute-done | bytes 516128 | tf_op jit(solution)/shard_map/ppermute | solution.py:143
  129.7 3.4 %fusion.315 = f32[288,512]{1,0:T(8,128)S(1)} fusion(bf16[288,3584]{1,0:T(8,128)(2,1)S(1)} %maximum_dynamic-update-slice_fusion.1, bf16[1,3584,512]{2,1,0:T(8,128)(2,1)} %param.14), kind=kOutput, calls=%fused_computation.497 | convolution fusion | flops 1056964608 | bytes 6324224 | tf_op jit(solution)/shard_map/dot_general | solution.py:212
  133.1 3.3 %fusion.337 = f32[288,512]{1,0:T(8,128)S(1)} fusion(bf16[288,3584]{1,0:T(8,128)(2,1)S(1)} %maximum_dynamic-update-slice_fusion.1, bf16[3584,512]{1,0:T(8,128)(2,1)} %collective-permute-done.6), kind=kOutput, calls=%fused_computation.514 | convolution fusion | flops 1056964608 | bytes 6324224 | tf_op jit(solution)/shard_map/dot_general | solution.py:212
  136.4 9.9 %collective-permute-done.13 = bf16[16,16128]{1,0:T(8,128)(2,1)S(1)} collective-permute-done((bf16[16,16128]{1,0:T(8,128)(2,1)S(1)}, bf16[16,16128]{1,0:T(8,128)(2,1)S(1)}, u32[]{:S(2)}, u32[]{:S(2)}) %collective-permute-start.13) | collective-permute-done | bytes 516128 | tf_op jit(solution)/shard_map/ppermute | solution.py:143
  149.2 3.4 %multiply_reduce_fusion.1 = (f32[288]{0:T(512)S(1)}, f32[288,512]{1,0:T(8,128)S(1)}) fusion(f32[288,512]{1,0:T(8,128)S(1)} %fusion.315, bf16[288,3584]{1,0:T(8,128)(2,1)S(1)} %maximum_dynamic-update-slice_fusion.2, bf16[1,512,3584]{2,1,0:T(8,128)(2,1)} %param.15), kind=kOutput, calls=%fused_computation.129 | convolution fusion | flops 1058144000 | bytes 6915200 | tf_op jit(solution)/shard_map/dot_general | solution.py:222
  152.7 3.4 %multiply_reduce_fusion = (f32[288]{0:T(512)S(1)}, f32[288,512]{1,0:T(8,128)S(1)}) fusion(f32[288,512]{1,0:T(8,128)S(1)} %fusion.337, bf16[288,3584]{1,0:T(8,128)(2,1)S(1)} %maximum_dynamic-update-slice_fusion.2, bf16[512,3584]{1,0:T(8,128)(2,1)} %collective-permute-done.7), kind=kOutput, calls=%fused_computation.127 | convolution fusion | flops 1058144000 | bytes 6915200 | tf_op jit(solution)/shard_map/dot_general | solution.py:222
  156.2 3.4 %fusion.111 = f32[288,3584]{1,0:T(8,128)S(1)} fusion(f32[288,512]{1,0:T(8,128)S(1)} %fusion.315, f32[288,512]{1,0:T(8,128)S(1)} %get-tuple-element.126, bf16[1,3584,512]{2,1,0:T(8,128)(2,1)} %param.14), kind=kOutput, calls=%fused_computation.182 | convolution fusion | flops 1058291712 | bytes 8978432 | tf_op jit(solution)/shard_map/dot_general | solution.py:227
  159.6 3.4 %fusion.1 = bf16[288,3584]{1,0:T(8,128)(2,1)S(1)} fusion(f32[288,3584]{1,0:T(8,128)S(1)} %fusion.111, bf16[3584,512]{1,0:T(8,128)(2,1)} %collective-permute-done.6, f32[288,512]{1,0:T(8,128)S(1)} %fusion.337, f32[288,512]{1,0:T(8,128)S(1)} %get-tuple-element.128), kind=kOutput, calls=%fused_computation.3 | convolution fusion | flops 1060356096 | bytes 11042816 | tf_op jit(solution)/shard_map/dot_general | solution.py:227
  168.7 1.9 collective-permute-start.9
  171.4 2.9 %collective-permute-start.16 = (bf16[16,16256]{1,0:T(8,128)(2,1)S(1)}, bf16[16,16256]{1,0:T(8,128)(2,1)S(1)}, u32[]{:S(2)}, u32[]{:S(2)}) collective-permute-start(bf16[16,16256]{1,0:T(8,128)(2,1)S(1)} %get-tuple-element.77), channel_id=1, source_target_pairs={{0,4},{1,5},{2,6},{3,7},{4,0},{5,1},{6,2},{7,3},{8,12},{9,13},{10,... | collective-permute-start | bytes 1560584 | tf_op jit(solution)/shard_map/ppermute | solution.py:143
  174.3 17.4 %collective-permute-done.10 = bf16[16,16128]{1,0:T(8,128)(2,1)S(1)} collective-permute-done((bf16[16,16128]{1,0:T(8,128)(2,1)S(1)}, bf16[16,16128]{1,0:T(8,128)(2,1)S(1)}, u32[]{:S(2)}, u32[]{:S(2)}) %collective-permute-start.10) | collective-permute-done | bytes 516128 | tf_op jit(solution)/shard_map/ppermute | solution.py:143
  193.3 32.1 %collective-permute-done.9 = bf16[16,16128]{1,0:T(8,128)(2,1)S(1)} collective-permute-done((bf16[16,16128]{1,0:T(8,128)(2,1)S(1)}, bf16[16,16128]{1,0:T(8,128)(2,1)S(1)}, u32[]{:S(2)}, u32[]{:S(2)}) %collective-permute-start.9) | collective-permute-done | bytes 516128 | tf_op jit(solution)/shard_map/ppermute | solution.py:143
  234.7 2.0 collective-permute-done.16
  236.7 11.4 %collective-permute-done.17 = bf16[16,16256]{1,0:T(8,128)(2,1)S(1)} collective-permute-done((bf16[16,16256]{1,0:T(8,128)(2,1)S(1)}, bf16[16,16256]{1,0:T(8,128)(2,1)S(1)}, u32[]{:S(2)}, u32[]{:S(2)}) %collective-permute-start.17) | collective-permute-done | bytes 520224 | tf_op jit(solution)/shard_map/ppermute | solution.py:143
  258.4 22.1 %collective-permute-done.18 = bf16[1,128,3584]{2,1,0:T(8,128)(2,1)S(1)} collective-permute-done((bf16[1,128,3584]{2,1,0:T(8,128)(2,1)S(1)}, bf16[1,128,3584]{2,1,0:T(8,128)(2,1)S(1)}, u32[]{:S(2)}, u32[]{:S(2)}) %collective-permute-start.18) | collective-permute-done | bytes 917536 | tf_op jit(solution)/shard_map/ppermute | solution.py:18
  (262 shorter events, 67.1 us)
Async XLA Ops:
  0.7 19.6 %copy-start.21 = (s32[64]{0:T(128)}, s32[64]{0:T(128)S(1)}, u32[]{:S(2)}) copy-start(s32[64]{0:T(128)S(1)} %get-tuple-element.136) | copy-start | bytes 772
  0.7 19.9 %copy-start.19 = (s32[64]{0:T(128)}, s32[64]{0:T(128)S(1)}, u32[]{:S(2)}) copy-start(s32[64]{0:T(128)S(1)} %get-tuple-element.135) | copy-start | bytes 772
  9.7 22.1 %collective-permute-start.3 = (bf16[16,16128]{1,0:T(8,128)(2,1)}, bf16[16,16128]{1,0:T(8,128)(2,1)S(1)}, u32[]{:S(2)}, u32[]{:S(2)}) collective-permute-start(bf16[16,16128]{1,0:T(8,128)(2,1)} %get-tuple-element.90), channel_id=1, source_target_pairs={{0,2},{1,3},{2,0},{3,1},{4,6},{5,7},{6,4},{7,5},{8,10},{9,11},{10,... | collective-permute-start | bytes 1548296 | tf_op jit(solution)/shard_map/ppermute | solution.py:143
  10.2 37.3 %collective-permute-start.4 = (bf16[16,16128]{1,0:T(8,128)(2,1)}, bf16[16,16128]{1,0:T(8,128)(2,1)}, u32[]{:S(2)}, u32[]{:S(2)}) collective-permute-start(bf16[16,16128]{1,0:T(8,128)(2,1)} %get-tuple-element.89), channel_id=1, source_target_pairs={{0,4},{1,5},{2,6},{3,7},{4,0},{5,1},{6,2},{7,3},{8,12},{9,13},{10,... | collective-permute-start | bytes 1548296 | tf_op jit(solution)/shard_map/ppermute | solution.py:143
  12.7 68.8 %collective-permute-start.5 = (bf16[16,16128]{1,0:T(8,128)(2,1)}, bf16[16,16128]{1,0:T(8,128)(2,1)}, u32[]{:S(2)}, u32[]{:S(2)}) collective-permute-start(bf16[16,16128]{1,0:T(8,128)(2,1)} %get-tuple-element.88), channel_id=1, source_target_pairs={{0,6},{1,7},{2,4},{3,5},{4,2},{5,3},{6,0},{7,1},{8,14},{9,15},{10,... | collective-permute-start | bytes 1548296 | tf_op jit(solution)/shard_map/ppermute | solution.py:143
  13.2 84.7 %collective-permute-start.6 = (bf16[3584,512]{1,0:T(8,128)(2,1)}, bf16[3584,512]{1,0:T(8,128)(2,1)}, u32[]{:S(2)}, u32[]{:S(2)}) collective-permute-start(bf16[3584,512]{1,0:T(8,128)(2,1)} %bitcast.7), channel_id=1, source_target_pairs={{0,1},{1,0},{2,3},{3,2},{4,5},{5,4},{6,7},{7,6},{8,9},{9,8},{10,11... | collective-permute-start | bytes 11010056 | tf_op jit(solution)/shard_map/ppermute | solution.py:12
  13.2 84.7 %collective-permute-start.7 = (bf16[512,3584]{1,0:T(8,128)(2,1)}, bf16[512,3584]{1,0:T(8,128)(2,1)}, u32[]{:S(2)}, u32[]{:S(2)}) collective-permute-start(bf16[512,3584]{1,0:T(8,128)(2,1)} %bitcast.8), channel_id=1, source_target_pairs={{0,1},{1,0},{2,3},{3,2},{4,5},{5,4},{6,7},{7,6},{8,9},{9,8},{10,11... | collective-permute-start | bytes 11010056 | tf_op jit(solution)/shard_map/ppermute | solution.py:12
  22.6 61.4 %copy-start.28 = (s32[32]{0:T(128)S(1)}, s32[32]{0:T(128)}, u32[]{:S(2)}) copy-start(s32[32]{0:T(128)} %broadcast_add_fusion) | copy-start | bytes 388
  22.6 60.5 %copy-start.33 = (s32[128,2]{0,1:T(2,128)}, s32[128,2]{0,1:T(2,128)S(1)}, u32[]{:S(2)}) copy-start(s32[128,2]{0,1:T(2,128)S(1)} %copy.59) | copy-start | bytes 3076
  23.4 62.4 %copy-start.31 = (s32[32]{0:T(128)}, s32[32]{0:T(128)S(1)}, u32[]{:S(2)}) copy-start(s32[32]{0:T(128)S(1)} %fusion.298) | copy-start | bytes 388
  31.8 76.7 %collective-permute-start = (bf16[16,16128]{1,0:T(8,128)(2,1)}, bf16[16,16128]{1,0:T(8,128)(2,1)}, u32[]{:S(2)}, u32[]{:S(2)}) collective-permute-start(bf16[16,16128]{1,0:T(8,128)(2,1)} %get-tuple-element.93), channel_id=1, source_target_pairs={{0,2},{1,3},{2,0},{3,1},{4,6},{5,7},{6,4},{7,5},{8,10},{9,11},{10,... | collective-permute-start | bytes 1548296 | tf_op jit(solution)/shard_map/ppermute | solution.py:143
  47.4 62.7 %collective-permute-start.1 = (bf16[16,16128]{1,0:T(8,128)(2,1)}, bf16[16,16128]{1,0:T(8,128)(2,1)}, u32[]{:S(2)}, u32[]{:S(2)}) collective-permute-start(bf16[16,16128]{1,0:T(8,128)(2,1)} %get-tuple-element.92), channel_id=1, source_target_pairs={{0,4},{1,5},{2,6},{3,7},{4,0},{5,1},{6,2},{7,3},{8,12},{9,13},{10,... | collective-permute-start | bytes 1548296 | tf_op jit(solution)/shard_map/ppermute | solution.py:143
  81.5 44.2 %collective-permute-start.2 = (bf16[16,16128]{1,0:T(8,128)(2,1)}, bf16[16,16128]{1,0:T(8,128)(2,1)}, u32[]{:S(2)}, u32[]{:S(2)}) collective-permute-start(bf16[16,16128]{1,0:T(8,128)(2,1)} %get-tuple-element.91), channel_id=1, source_target_pairs={{0,6},{1,7},{2,4},{3,5},{4,2},{5,3},{6,0},{7,1},{8,14},{9,15},{10,... | collective-permute-start | bytes 1548296 | tf_op jit(solution)/shard_map/ppermute | solution.py:143
  97.9 38.6 %collective-permute-start.11 = (bf16[16,16128]{1,0:T(8,128)(2,1)}, bf16[16,16128]{1,0:T(8,128)(2,1)}, u32[]{:S(2)}, u32[]{:S(2)}) collective-permute-start(bf16[16,16128]{1,0:T(8,128)(2,1)} %get-tuple-element.81), channel_id=1, source_target_pairs={{0,2},{1,3},{2,0},{3,1},{4,6},{5,7},{6,4},{7,5},{8,10},{9,11},{10,... | collective-permute-start | bytes 1548296 | tf_op jit(solution)/shard_map/ppermute | solution.py:143
  97.9 38.6 %collective-permute-start.12 = (bf16[16,16128]{1,0:T(8,128)(2,1)}, bf16[16,16128]{1,0:T(8,128)(2,1)}, u32[]{:S(2)}, u32[]{:S(2)}) collective-permute-start(bf16[16,16128]{1,0:T(8,128)(2,1)} %get-tuple-element.80), channel_id=1, source_target_pairs={{0,4},{1,5},{2,6},{3,7},{4,0},{5,1},{6,2},{7,3},{8,12},{9,13},{10,... | collective-permute-start | bytes 1548296 | tf_op jit(solution)/shard_map/ppermute | solution.py:143
  108.5 37.9 %collective-permute-start.13 = (bf16[16,16128]{1,0:T(8,128)(2,1)S(1)}, bf16[16,16128]{1,0:T(8,128)(2,1)S(1)}, u32[]{:S(2)}, u32[]{:S(2)}) collective-permute-start(bf16[16,16128]{1,0:T(8,128)(2,1)S(1)} %copy-done.12), channel_id=1, source_target_pairs={{0,6},{1,7},{2,4},{3,5},{4,2},{5,3},{6,0},{7,1},{8,14},{9,15},{10,... | collective-permute-start | bytes 1548296 | tf_op jit(solution)/shard_map/ppermute | solution.py:143
  167.1 24.6 %collective-permute-start.10 = (bf16[16,16128]{1,0:T(8,128)(2,1)S(1)}, bf16[16,16128]{1,0:T(8,128)(2,1)S(1)}, u32[]{:S(2)}, u32[]{:S(2)}) collective-permute-start(bf16[16,16128]{1,0:T(8,128)(2,1)S(1)} %get-tuple-element.83), channel_id=1, source_target_pairs={{0,6},{1,7},{2,4},{3,5},{4,2},{5,3},{6,0},{7,1},{8,14},{9,15},{10,... | collective-permute-start | bytes 1548296 | tf_op jit(solution)/shard_map/ppermute | solution.py:143
  168.7 24.5 %collective-permute-start.8 = (bf16[16,16128]{1,0:T(8,128)(2,1)S(1)}, bf16[16,16128]{1,0:T(8,128)(2,1)S(1)}, u32[]{:S(2)}, u32[]{:S(2)}) collective-permute-start(bf16[16,16128]{1,0:T(8,128)(2,1)S(1)} %get-tuple-element.85), channel_id=1, source_target_pairs={{0,2},{1,3},{2,0},{3,1},{4,6},{5,7},{6,4},{7,5},{8,10},{9,11},{10,... | collective-permute-start | bytes 1548296 | tf_op jit(solution)/shard_map/ppermute | solution.py:143
  168.7 56.6 %collective-permute-start.9 = (bf16[16,16128]{1,0:T(8,128)(2,1)S(1)}, bf16[16,16128]{1,0:T(8,128)(2,1)S(1)}, u32[]{:S(2)}, u32[]{:S(2)}) collective-permute-start(bf16[16,16128]{1,0:T(8,128)(2,1)S(1)} %get-tuple-element.84), channel_id=1, source_target_pairs={{0,4},{1,5},{2,6},{3,7},{4,0},{5,1},{6,2},{7,3},{8,12},{9,13},{10,... | collective-permute-start | bytes 1548296 | tf_op jit(solution)/shard_map/ppermute | solution.py:143
  171.1 63.6 %collective-permute-start.15 = (bf16[16,16256]{1,0:T(8,128)(2,1)S(1)}, bf16[16,16256]{1,0:T(8,128)(2,1)S(1)}, u32[]{:S(2)}, u32[]{:S(2)}) collective-permute-start(bf16[16,16256]{1,0:T(8,128)(2,1)S(1)} %get-tuple-element.78), channel_id=1, source_target_pairs={{0,2},{1,3},{2,0},{3,1},{4,6},{5,7},{6,4},{7,5},{8,10},{9,11},{10,... | collective-permute-start | bytes 1560584 | tf_op jit(solution)/shard_map/ppermute | solution.py:143
  171.4 65.3 %collective-permute-start.16 = (bf16[16,16256]{1,0:T(8,128)(2,1)S(1)}, bf16[16,16256]{1,0:T(8,128)(2,1)S(1)}, u32[]{:S(2)}, u32[]{:S(2)}) collective-permute-start(bf16[16,16256]{1,0:T(8,128)(2,1)S(1)} %get-tuple-element.77), channel_id=1, source_target_pairs={{0,4},{1,5},{2,6},{3,7},{4,0},{5,1},{6,2},{7,3},{8,12},{9,13},{10,... | collective-permute-start | bytes 1560584 | tf_op jit(solution)/shard_map/ppermute | solution.py:143
  191.6 56.5 %collective-permute-start.17 = (bf16[16,16256]{1,0:T(8,128)(2,1)S(1)}, bf16[16,16256]{1,0:T(8,128)(2,1)S(1)}, u32[]{:S(2)}, u32[]{:S(2)}) collective-permute-start(bf16[16,16256]{1,0:T(8,128)(2,1)S(1)} %get-tuple-element.76), channel_id=1, source_target_pairs={{0,6},{1,7},{2,4},{3,5},{4,2},{5,3},{6,0},{7,1},{8,14},{9,15},{10,... | collective-permute-start | bytes 1560584 | tf_op jit(solution)/shard_map/ppermute | solution.py:143
  232.9 25.5 %collective-permute-start.14 = (bf16[1,128,3584]{2,1,0:T(8,128)(2,1)S(1)}, bf16[1,128,3584]{2,1,0:T(8,128)(2,1)S(1)}, u32[]{:S(2)}, u32[]{:S(2)}) collective-permute-start(bf16[1,128,3584]{2,1,0:T(8,128)(2,1)S(1)} %fusion.20), channel_id=1, source_target_pairs={{24,0},{0,8},{8,16},{16,24},{25,1},{1,9},{9,17},{17,25},{26,2},{2,... | collective-permute-start | bytes 2752520 | tf_op jit(solution)/shard_map/ppermute | solution.py:18
  257.8 22.7 %collective-permute-start.18 = (bf16[1,128,3584]{2,1,0:T(8,128)(2,1)S(1)}, bf16[1,128,3584]{2,1,0:T(8,128)(2,1)S(1)}, u32[]{:S(2)}, u32[]{:S(2)}) collective-permute-start(bf16[1,128,3584]{2,1,0:T(8,128)(2,1)S(1)} %fusion.70), channel_id=1, source_target_pairs={{8,0},{16,8},{24,16},{0,24},{9,1},{17,9},{25,17},{1,25},{10,2},{18... | collective-permute-start | bytes 2752520 | tf_op jit(solution)/shard_map/ppermute | solution.py:18
  (39 other events, 168.8 us)
